TPU v7x, 32 devices: a whole 2x2x4 slice. The times are simulated.
32 devices in a mesh: dp: 4 (over y, x), row: 4 (over z), col: 2 (over core).
Axes of the slice: x: 2, y: 2, z: 4, core: 2. Of those that a mesh axis runs over, the one named last changes fastest.
Arguments:
- tokens: bfloat16 [1088, 4096], P('row', ('dp', 'col')), may hold values from -6 to 6
- block_order: int32 [4, 16], P('dp'), may hold values from 0 to 15, each once within a row
- first_gain: float32 [1088], P('row'), may hold values from 0.25 to 1.75
- first_shift: float32 [1088], P('row'), may hold values from -4 to 4
- qkv_weight: bfloat16 [1088, 3264], P('row', 'col'), may hold values from -0.1875 to 0.1875
- query_value_bias: float32 [2, 1088], replicated, may hold values from -4 to 4
- output_weight: bfloat16 [1088, 1088], P('col', 'row'), may hold values from -0.5 to 0.5
- output_bias: float32 [1088], P('row'), may hold values from -4 to 4
- second_gain: float32 [1088], P('row'), may hold values from 0.25 to 1.75
- second_shift: float32 [1088], P('row'), may hold values from -4 to 4
- up_weight: bfloat16 [1088, 4352], P('row', 'col'), may hold values from -0.1875 to 0.1875
- up_bias: float32 [4352], P('col'), may hold values from -4 to 4
- down_weight: bfloat16 [1088, 4352], P('row', 'col'), may hold values from -0.09375 to 0.09375
- down_bias: float32 [1088], P('row'), may hold values from -4 to 4
- cotangent: bfloat16 [1088, 4096], P('row', ('dp', 'col')), may hold values from -6 to 6
Outputs:
- result: bfloat16 [1088, 4096], P('row', ('dp', 'col'))
- input_grad: float32 [1088, 4096], P('row', ('dp', 'col'))
- first_gain_grad: float32 [1088], replicated
- first_shift_grad: float32 [1088], replicated
- qkv_weight_grad: float32 [1088, 3264], P('row', 'col')
- query_value_bias_grad: float32 [2, 1088], replicated
- output_weight_grad: float32 [1088, 1088], P('col', 'row')
- output_bias_grad: float32 [1088], replicated
- second_gain_grad: float32 [1088], replicated
- second_shift_grad: float32 [1088], replicated
- up_weight_grad: float32 [1088, 4352], P('row', 'col')
- up_bias_grad: float32 [4352], replicated
- down_weight_grad: float32 [1088, 4352], P('row', 'col')
- down_bias_grad: float32 [1088], replicated
Inputs may be any that keep to these rules, and one draw needn't show every extreme that they name: Each row names every position block once: stored block b of a sequence holds that sequence's positions block_order[s, b] * 64 to block_order[s, b] * 64 + 63.
All inputs are finite; a program needn't handle non-finite values.
Results may differ from a plain program's by a relative error of at most 0.011.
Values may be sent and summed in bfloat16 or wider, within the bound.
No kernel may reach another device: no remote copies, remote signals or barrier semaphores. Data moves between devices by JAX's collectives and lax.ppermute only.
A program may use at most 320 MiB of HBM per device.

v0:
```python
import jax
import jax.numpy as jnp
from jax import lax
from jax.sharding import PartitionSpec as P

D = 1088
HEADS = 17
HEAD_DIM = 64
FF = 4352
SEQS = 1


epsilon = 1e-05


def gelu_exact(before):
    return jax.nn.gelu(before, approximate=False)


def contract(left_side, right_side, flipped):
    if flipped:
        return lax.dot_general(
            left_side, right_side, (((1,), (1,)), ((), ())), preferred_element_type=jnp.float32
        )
    return jnp.dot(left_side, right_side, preferred_element_type=jnp.float32)


def outer_sum(left_side, right_side):
    return lax.dot_general(
        left_side, right_side, (((0,), (0,)), ((), ())), preferred_element_type=jnp.float32
    )


def gather_columns(values):
    return lax.all_gather(values, "col", axis=0, tiled=True)


def gather_rows(values):
    return lax.all_gather(values, "row", axis=0, tiled=True)


def width_product(left_side, weight, flipped):
    return lax.psum_scatter(
        contract(left_side, weight, flipped), "row", scatter_dimension=0, tiled=True
    )


def col_partial(left_side, weight, flipped):
    return lax.psum_scatter(
        contract(left_side, weight, flipped), "col", scatter_dimension=0, tiled=True
    )


def to_heads(values):
    return lax.all_to_all(values, "col", split_axis=0, concat_axis=1, tiled=True)


def from_heads(values):
    return lax.all_to_all(values, "col", split_axis=1, concat_axis=0, tiled=True)


def row_pair(first_sum, second_sum):
    return lax.psum((first_sum, second_sum), "row")


def row_single(values):
    return lax.psum(values, "row")


def norm_forward(hidden, norm_gain, norm_shift):
    average = row_single(jnp.sum(hidden, 1)) / D
    centered = hidden - average[:, None]
    variance = row_single(jnp.sum(centered * centered, 1)) / D
    inverse = lax.rsqrt(variance + epsilon)
    normal = centered * inverse[:, None]
    return ((normal * norm_gain + norm_shift).astype(jnp.bfloat16), normal, inverse)


def norm_backward(upstream, normal, inverse, norm_gain):
    scaled = upstream * norm_gain
    first_sum, second_sum = row_pair(jnp.sum(scaled, 1), jnp.sum(scaled * normal, 1))
    return inverse[:, None] * (scaled - first_sum[:, None] / D - normal * (second_sum[:, None] / D))


def widen(piece_sum, full_width, slot_index):
    return lax.dynamic_update_slice_in_dim(
        jnp.zeros((full_width,), jnp.float32), piece_sum, slot_index * piece_sum.shape[0], 0
    )


def shards(
    tokens,
    block_order,
    first_gain,
    first_shift,
    qkv_weight,
    query_value_bias,
    output_weight,
    output_bias,
    second_gain,
    second_shift,
    up_weight,
    up_bias,
    down_weight,
    down_bias,
    cotangent,
):
    row_index = lax.axis_index("row")
    col_index = lax.axis_index("col")
    col_total = lax.axis_size("col")
    group_rows = tokens.shape[1] * col_total
    seq_length = group_rows // SEQS
    query_rows = group_rows // (lax.axis_size("row") * col_total)
    block_size = seq_length // block_order.shape[1]
    scale_factor = HEAD_DIM ** (-0.5)
    inputs = tokens.T.astype(jnp.float32)
    upstream_rows = cotangent.T
    order_flat = block_order.reshape(-1)
    places = (
        jnp.broadcast_to(order_flat[:, None], (order_flat.shape[0], block_size)) * block_size
        + jnp.arange(block_size, dtype=jnp.int32)[None, :]
    ).reshape(-1)
    sequence_floor = jnp.arange(group_rows, dtype=jnp.int32) // seq_length * seq_length
    key_rank = sequence_floor + places
    query_start = (row_index * col_total + col_index) * query_rows
    query_rank = lax.dynamic_slice_in_dim(key_rank, query_start, query_rows)
    query_floor = lax.dynamic_slice_in_dim(sequence_floor, query_start, query_rows)
    allowed = (key_rank[None, :] <= query_rank[:, None]) & (
        key_rank[None, :] >= query_floor[:, None]
    )
    first_normed, first_normal, first_inverse = norm_forward(inputs, first_gain, first_shift)
    first_all = gather_columns(first_normed)
    part_width = qkv_weight.shape[1]
    bias_row = jnp.concatenate(
        [query_value_bias[0], jnp.zeros_like(query_value_bias[0]), query_value_bias[1]]
    )
    local_bias = lax.dynamic_slice_in_dim(bias_row, col_index * part_width, part_width)
    projected = (width_product(first_all, qkv_weight, False) + local_bias).astype(jnp.bfloat16)
    heads_in = to_heads(projected)
    queries = heads_in[:, :D].reshape(query_rows, HEADS, HEAD_DIM)
    keys_all, values_all = (
        lax.all_gather(heads_in[:, D : 2 * D], ("row", "col"), axis=0, tiled=True),
        lax.all_gather(heads_in[:, 2 * D :], ("row", "col"), axis=0, tiled=True),
    )
    keys_all = keys_all.reshape(group_rows, HEADS, HEAD_DIM)
    values_all = values_all.reshape(group_rows, HEADS, HEAD_DIM)

    def scores_of():
        raw_scores = (
            jnp.einsum("qhd,khd->hqk", queries, keys_all, preferred_element_type=jnp.float32)
            * scale_factor
        )
        return jnp.where(allowed[None], raw_scores, -1e30)

    scores = scores_of()
    largest = jnp.max(scores, 2, keepdims=True)
    powers = jnp.exp(scores - largest)
    totals = jnp.sum(powers, 2, keepdims=True)
    log_total = largest + jnp.log(totals)
    attention_weights = (powers / totals).astype(jnp.bfloat16)
    attended = jnp.einsum(
        "hqk,khd->qhd", attention_weights, values_all, preferred_element_type=jnp.float32
    )
    attended = attended.reshape(query_rows, D).astype(jnp.bfloat16)
    attended_all = gather_rows(from_heads(attended))
    middle = inputs + col_partial(attended_all, output_weight, False) + output_bias
    second_normed, second_normal, second_inverse = norm_forward(middle, second_gain, second_shift)
    second_all = gather_columns(second_normed)
    before = width_product(second_all, up_weight, False) + up_bias
    hidden_all = gather_rows(gelu_exact(before).astype(jnp.bfloat16))
    result = (middle + col_partial(hidden_all, down_weight, True) + down_bias).astype(jnp.bfloat16)
    grad_out_all = gather_columns(upstream_rows)
    down_weight_grad = outer_sum(grad_out_all, hidden_all)
    down_bias_part = jnp.sum(upstream_rows.astype(jnp.float32), 0)
    grad_hidden = width_product(grad_out_all, down_weight, False)
    grad_before = jax.vjp(gelu_exact, before)[1](grad_hidden)[0].astype(jnp.bfloat16)
    up_bias_part = jnp.sum(grad_before.astype(jnp.float32), 0)
    grad_before_all = gather_rows(grad_before)
    up_weight_grad = outer_sum(second_all, grad_before_all)
    grad_second = col_partial(grad_before_all, up_weight, True)
    second_gain_part = jnp.sum(grad_second * second_normal, 0)
    second_shift_part = jnp.sum(grad_second, 0)
    grad_middle = upstream_rows.astype(jnp.float32) + norm_backward(
        grad_second, second_normal, second_inverse, second_gain
    )
    grad_branch = grad_middle.astype(jnp.bfloat16)
    output_bias_part = jnp.sum(grad_branch.astype(jnp.float32), 0)
    grad_branch_all = gather_columns(grad_branch)
    output_weight_grad = outer_sum(attended_all, grad_branch_all)
    grad_attended = to_heads(
        width_product(grad_branch_all, output_weight, True).astype(jnp.bfloat16)
    )
    grad_attended = grad_attended.reshape(query_rows, HEADS, HEAD_DIM)
    scores = scores_of()
    probability = jnp.exp(scores - log_total)
    value_part = jnp.einsum(
        "hqk,qhd->khd",
        probability.astype(jnp.bfloat16),
        grad_attended,
        preferred_element_type=jnp.float32,
    )
    grad_probs = jnp.einsum(
        "qhd,khd->hqk", grad_attended, values_all, preferred_element_type=jnp.float32
    )
    inner_sum = jnp.sum(probability * grad_probs, 2, keepdims=True)
    grad_scores = (probability * (grad_probs - inner_sum)).astype(jnp.bfloat16)
    grad_queries = (
        jnp.einsum("hqk,khd->qhd", grad_scores, keys_all, preferred_element_type=jnp.float32)
        * scale_factor
    )
    key_part = (
        jnp.einsum("hqk,qhd->khd", grad_scores, queries, preferred_element_type=jnp.float32)
        * scale_factor
    )
    grad_keys, grad_values = (
        lax.psum_scatter(
            key_part.reshape(group_rows, D), ("row", "col"), scatter_dimension=0, tiled=True
        ),
        lax.psum_scatter(
            value_part.reshape(group_rows, D), ("row", "col"), scatter_dimension=0, tiled=True
        ),
    )
    grad_heads = jnp.concatenate(
        [
            grad_queries.reshape(query_rows, D).astype(jnp.bfloat16),
            grad_keys.astype(jnp.bfloat16),
            grad_values.astype(jnp.bfloat16),
        ],
        1,
    )
    query_bias_part = jnp.sum(grad_heads[:, :D].astype(jnp.float32), 0)
    value_bias_part = jnp.sum(grad_heads[:, 2 * D :].astype(jnp.float32), 0)
    grad_projected_all = gather_rows(from_heads(grad_heads))
    qkv_weight_grad = outer_sum(first_all, grad_projected_all)
    grad_first = col_partial(grad_projected_all, qkv_weight, True)
    first_gain_part = jnp.sum(grad_first * first_normal, 0)
    first_shift_part = jnp.sum(grad_first, 0)
    input_grad = grad_middle + norm_backward(grad_first, first_normal, first_inverse, first_gain)
    qkv_weight_grad, output_weight_grad, up_weight_grad, down_weight_grad = lax.psum(
        (qkv_weight_grad, output_weight_grad, up_weight_grad, down_weight_grad), "dp"
    )
    stacked = jnp.stack(
        [
            widen(first_gain_part, D, row_index),
            widen(first_shift_part, D, row_index),
            widen(output_bias_part, D, row_index),
            widen(second_gain_part, D, row_index),
            widen(second_shift_part, D, row_index),
            widen(down_bias_part, D, row_index),
            query_bias_part,
            value_bias_part,
        ]
    )
    stacked, up_full = lax.psum((stacked, widen(up_bias_part, FF, col_index)), ("dp", "row", "col"))
    return (
        result.T,
        input_grad.T,
        stacked[0],
        stacked[1],
        qkv_weight_grad,
        stacked[6:8],
        output_weight_grad,
        stacked[2],
        stacked[3],
        stacked[4],
        up_weight_grad,
        up_full,
        down_weight_grad,
        stacked[5],
    )


def solution(mesh):
    placed = (
        P("row", ("dp", "col")),
        P("dp", None),
        P("row"),
        P("row"),
        P("row", "col"),
        P(),
        P("col", "row"),
        P("row"),
        P("row"),
        P("row"),
        P("row", "col"),
        P("col"),
        P("row", "col"),
        P("row"),
        P("row", ("dp", "col")),
    )
    return jax.shard_map(
        shards,
        mesh=mesh,
        in_specs=placed,
        out_specs=(
            P("row", ("dp", "col")),
            P("row", ("dp", "col")),
            P(),
            P(),
            P("row", "col"),
            P(),
            P("col", "row"),
            P(),
            P(),
            P(),
            P("row", "col"),
            P(),
            P("row", "col"),
            P(),
        ),
        check_vma=False,
    )
```

profile of v0, /device:TPU:0, one launch (start us, length us, event | category | flops | bytes accessed | tf_op | source)
XLA Modules:
  0.0 1237.4 jit_solution(11326881429415198663)
XLA Ops:
  8.3 13.4 %psum.98 = f32[512]{0:T(512)S(1)} all-reduce(f32[512]{0:T(512)S(1)} %convert_reduce_fusion.2), channel_id=1, replica_groups=mesh['dp'=4,'row'=4,'col'=2] {'row'}, use_global_device_ids=true, to_apply=%region_1.2 | all-reduce | flops 512 | bytes 4096 | tf_op jit(solution)/shard_map/psum | solution.py:67
  22.9 8.4 psum.99
  31.2 1.1 fusion.24
  32.4 2.2 all_gather.30
  34.6 5.9 fusion.46
  41.4 116.1 %reduce-scatter.11.cloned.1.call-done = f32[256,1632]{0,1:T(8,128)} async-done(((f32[1024,1632]{0,1:T(8,128)}), f32[256,1632]{0,1:T(8,128)}) %reduce-scatter.11.cloned.1.call-update) | async-done | bytes 1671184 | tf_op jit(solution)/shard_map/reduce_scatter | solution.py:43
  157.4 1.7 copy_bitcast_fusion
  159.2 4.4 all_to_all.70
  165.8 31.2 %all-gather.9.cloned.1.call-done = bf16[1024,1088]{0,1:T(8,128)(2,1)} async-done(((bf16[128,1088]{0,1:T(8,128)(2,1)}), bf16[1024,1088]{0,1:T(8,128)(2,1)}) %all-gather.9.cloned.1.call-update) | async-done | bytes 2228240 | tf_op jit(solution)/shard_map/all_gather | solution.py:142
  197.0 3.4 fusion.45
  200.3 3.4 copy-done.2
  203.8 2.0 fusion
  205.7 24.3 %all-gather.7.cloned.1.call-done = bf16[1024,1088]{0,1:T(8,128)(2,1)} async-done(((bf16[128,1088]{0,1:T(8,128)(2,1)}), bf16[1024,1088]{0,1:T(8,128)(2,1)}) %all-gather.7.cloned.1.call-update) | async-done | bytes 2228240 | tf_op jit(solution)/shard_map/all_gather | solution.py:143
  230.0 6.2 fusion.13
  236.1 3.9 all_to_all.71
  240.9 30.2 %all-gather.11.cloned.1.call-done = bf16[1024,544]{0,1:T(8,128)(2,1)} async-done(((bf16[256,544]{0,1:T(8,128)(2,1)}), bf16[1024,544]{0,1:T(8,128)(2,1)}) %all-gather.11.cloned.1.call-update) | async-done | bytes 1114128 | tf_op jit(solution)/shard_map/all_gather | solution.py:39
  271.0 2.9 fusion.56
  274.0 2.2 all_gather.36
  276.2 6.4 fusion.49
  283.5 1.2 fusion.42
  284.7 11.1 psum.100
  295.9 8.6 psum.101
  304.7 2.4 all_gather.34
  307.9 5.0 fusion.47
  312.9 124.8 %reduce-scatter.19.cloned.1.call-done = f32[256,2176]{1,0:T(8,128)} async-done(((f32[1024,2176]{1,0:T(8,128)}), f32[256,2176]{1,0:T(8,128)}) %reduce-scatter.19.cloned.1.call-update) | async-done | bytes 2228240 | tf_op jit(solution)/shard_map/reduce_scatter | solution.py:43
  437.7 155.9 %reduce-scatter.15.cloned.1.call-done = f32[256,2176]{1,0:T(8,128)} async-done(((f32[1024,2176]{1,0:T(8,128)}), f32[256,2176]{1,0:T(8,128)}) %reduce-scatter.15.cloned.1.call-update) | async-done | bytes 2228240 | tf_op jit(solution)/shard_map/reduce_scatter | solution.py:43
  593.6 8.0 convert_reduce_fusion
  601.7 86.1 %all-gather.15.cloned.1.call-done = bf16[1024,2176]{1,0:T(8,128)(2,1)} async-done(((bf16[256,2176]{1,0:T(8,128)(2,1)}), bf16[1024,2176]{1,0:T(8,128)(2,1)}) %all-gather.15.cloned.1.call-update) | async-done | bytes 4456464 | tf_op jit(solution)/shard_map/all_gather | solution.py:39
  687.8 4.7 fusion.50
  692.6 7.2 reduce-scatter.21.cloned.1.call-done
  699.8 1.4 multiply_reduce_fusion.1
  701.2 11.9 all-reduce.2
  713.1 1.4 convert_reduce_fusion.5
  714.5 2.2 all_gather.38
  716.7 2.2 fusion.51
  719.0 44.2 %reduce-scatter.23.cloned.1.call-done = f32[256,544]{0,1:T(8,128)} async-done(((f32[1024,544]{0,1:T(8,128)}), f32[256,544]{0,1:T(8,128)}) %reduce-scatter.23.cloned.1.call-update) | async-done | bytes 557072 | tf_op jit(solution)/shard_map/reduce_scatter | solution.py:43
  764.3 3.9 all_to_all.72
  768.2 7.3 fusion.2
  775.6 6.7 multiply_reduce_fusion
  782.3 4.6 multiply_convert_fusion
  786.9 3.2 broadcast_multiply_fusion
  790.7 4.7 convert_reduce_fusion.4
  795.4 32.2 %reduce-scatter.27.cloned.1.call-done = f32[128,1088]{0,1:T(8,128)} async-done(((f32[1024,1088]{0,1:T(8,128)}), f32[128,1088]{0,1:T(8,128)}) %reduce-scatter.27.cloned.1.call-update) | async-done | bytes 557072 | tf_op jit(solution)/shard_map/reduce_scatter | solution.py:219
  827.6 1.3 convert_reduce_fusion.3
  828.9 51.5 %reduce-scatter.25.cloned.1.call-done = f32[128,1088]{0,1:T(8,128)} async-done(((f32[1024,1088]{0,1:T(8,128)}), f32[128,1088]{0,1:T(8,128)}) %reduce-scatter.25.cloned.1.call-update) | async-done | bytes 557072 | tf_op jit(solution)/shard_map/reduce_scatter | solution.py:216
  881.5 4.4 all_to_all.73
  885.9 1.3 copy.40
  887.2 3.6 multiply_convert_fusion.1
  890.9 62.5 %all-gather.17.cloned.1.call-done = bf16[1024,1632]{1,0:T(8,128)(2,1)} async-done(((bf16[256,1632]{1,0:T(8,128)(2,1)}), bf16[1024,1632]{1,0:T(8,128)(2,1)}) %all-gather.17.cloned.1.call-update) | async-done | bytes 3342352 | tf_op jit(solution)/shard_map/all_gather | solution.py:39
  953.4 4.4 fusion.52
  957.8 81.3 %all-gather.13.cloned.1.call-done = bf16[1024,2176]{1,0:T(8,128)(2,1)} async-done(((bf16[256,2176]{1,0:T(8,128)(2,1)}), bf16[1024,2176]{1,0:T(8,128)(2,1)}) %all-gather.13.cloned.1.call-update) | async-done | bytes 4456464 | tf_op jit(solution)/shard_map/all_gather | solution.py:39
  1039.1 5.1 fusion.48
  1044.3 5.6 convolution_bitcast_fusion
  1049.9 5.3 fusion.55
  1055.1 1.5 fusion.54
  1056.6 2.4 fusion.53
  1060.1 1.4 fusion.30
  1061.5 9.1 all-reduce.1
  1070.7 2.8 fusion.29
  1074.2 41.8 %all-reduce = (f32[8,1088]{1,0:T(8,128)S(1)}, f32[4352]{0:T(1024)}) all-reduce(f32[8,1088]{1,0:T(8,128)S(1)} %stack.38, f32[4352]{0:T(1024)S(1)} %dynamic_update_slice.33), channel_id=1, replica_groups=mesh['dp'=4,'row'=4,'col'=2] {'dp','row','col'}, use_global_device_ids=true, to_apply=%region_37.38 | all-reduce | flops 13056 | bytes 104448 | tf_op jit(solution)/shard_map/psum | solution.py:254
  1117.2 105.9 %all-reduce.6.cloned.1.call-done = (f32[272,1632]{1,0:T(8,128)}, f32[544,272]{0,1:T(8,128)}, f32[272,2176]{1,0:T(8,128)}, f32[272,2176]{1,0:T(8,128)}) async-done(((f32[272,1632]{1,0:T(8,128)}, f32[544,272]{0,1:T(8,128)}, f32[272,2176]{1,0:T(8,128)}, f32[272,2176]{1,0:T(8,128)}), (f32[272,1632]{1,0:T(8,128)}, f32[544,272]{0,1:T(8,128)}, f32[272,2176]{1,0:T(8,128)}, ...) | async-done | bytes 7102480 | tf_op jit(solution)/shard_map/psum | solution.py:239
  1223.1 3.0 copy.58
  1226.9 1.4 copy.60
  1229.4 1.4 copy.61
  (145 shorter events, 16.2 us)
Async XLA Ops:
  7.2 300.7 %copy-start = (bf16[272,2176]{1,0:T(8,128)(2,1)S(1)}, bf16[272,2176]{1,0:T(8,128)(2,1)}, u32[]{:S(2)}) copy-start(bf16[272,2176]{1,0:T(8,128)(2,1)} %param.25) | copy-start | bytes 3551236
  7.2 150.2 %reduce-scatter.11.cloned.1.call-start = ((), (), s32[]{:S(2)}) async-start(), calls=%async_computation.14 | async-start | bytes 8355840 | tf_op jit(solution)/shard_map/reduce_scatter | solution.py:43
  40.5 0.7 copy-start.21
  40.5 156.5 %all-gather.9.cloned.1.call-start = ((), (), s32[]{:S(2)}) async-start(), calls=%async_computation.16 | async-start | bytes 2506752 | tf_op jit(solution)/shard_map/all_gather | solution.py:142
  159.2 6.1 copy-start.26
  164.5 65.5 %all-gather.7.cloned.1.call-start = ((), (), s32[]{:S(2)}) async-start(), calls=%async_computation.15 | async-start | bytes 2506752 | tf_op jit(solution)/shard_map/all_gather | solution.py:143
  165.2 105.8 %all-gather.11.cloned.1.call-start = ((), (), s32[]{:S(2)}) async-start(), calls=%async_computation.17 | async-start | bytes 1392640 | tf_op jit(solution)/shard_map/all_gather | solution.py:39
  200.3 3.4 copy-start.2
  230.0 41.1 %copy-start.15 = (bf16[544,272]{0,1:T(8,128)(2,1)S(1)}, bf16[544,272]{0,1:T(8,128)(2,1)}, u32[]{:S(2)}) copy-start(bf16[544,272]{0,1:T(8,128)(2,1)} %param.21) | copy-start | bytes 887812
  240.1 33.9 %copy-start.7 = (bf16[272,512]{1,0:T(8,128)(2,1)S(1)}, bf16[272,512]{1,0:T(8,128)(2,1)}, u32[]{:S(2)}) copy-start(bf16[272,512]{1,0:T(8,128)(2,1)} %param.29) | copy-start | bytes 835588
  240.8 41.8 %reduce-scatter.13.cloned.1.call-start = ((), (), s32[]{:S(2)}) async-start(), calls=%async_computation.18 | async-start | bytes 1671168 | tf_op jit(solution)/shard_map/reduce_scatter | solution.py:49
  273.9 163.8 %reduce-scatter.19.cloned.1.call-start = ((), (), s32[]{:S(2)}) async-start(), calls=%async_computation.22 | async-start | bytes 11141120 | tf_op jit(solution)/shard_map/reduce_scatter | solution.py:43
  276.2 6.4 copy-start.11
  282.6 1.0 copy-start.4
  282.6 1.0 copy-start.23
  282.6 22.0 %copy-start.19 = (f32[272]{0:T(512)S(1)}, f32[272]{0:T(512)}, u32[]{:S(2)}) copy-start(f32[272]{0:T(512)} %param.23) | copy-start | bytes 3268
  282.6 22.0 %copy-start.24 = (f32[272]{0:T(512)S(1)}, f32[272]{0:T(512)}, u32[]{:S(2)}) copy-start(f32[272]{0:T(512)} %param.24) | copy-start | bytes 3268
  282.6 311.0 %reduce-scatter.15.cloned.1.call-start = ((), (), s32[]{:S(2)}) async-start(), calls=%async_computation.19 | async-start | bytes 11141120 | tf_op jit(solution)/shard_map/reduce_scatter | solution.py:43
  307.1 0.8 copy-start.13
  312.9 280.8 %copy-start.18 = (f32[2176]{0:T(1024)S(1)}, f32[2176]{0:T(1024)}, u32[]{:S(2)}) copy-start(f32[2176]{0:T(1024)} %param.26) | copy-start | bytes 26116
  312.9 374.9 %all-gather.15.cloned.1.call-start = ((), (), s32[]{:S(2)}) async-start(), calls=%async_computation.23 | async-start | bytes 5570560 | tf_op jit(solution)/shard_map/all_gather | solution.py:39
  601.7 98.1 %reduce-scatter.21.cloned.1.call-start = ((), (), s32[]{:S(2)}) async-start(), calls=%async_computation.24 | async-start | bytes 1671168 | tf_op jit(solution)/shard_map/reduce_scatter | solution.py:49
  692.6 24.2 %copy-start.16 = (bf16[544,272]{0,1:T(8,128)(2,1)S(1)}, bf16[544,272]{0,1:T(8,128)(2,1)}, u32[]{:S(2)}) copy-start(bf16[544,272]{0,1:T(8,128)(2,1)} %param.21) | copy-start | bytes 887812
  692.6 70.6 %reduce-scatter.23.cloned.1.call-start = ((), (), s32[]{:S(2)}) async-start(), calls=%async_computation.25 | async-start | bytes 2785280 | tf_op jit(solution)/shard_map/reduce_scatter | solution.py:43
  718.9 108.6 %reduce-scatter.27.cloned.1.call-start = ((), (), s32[]{:S(2)}) async-start(), calls=%async_computation.27 | async-start | bytes 5013504 | tf_op jit(solution)/shard_map/reduce_scatter | solution.py:219
  775.5 104.8 %reduce-scatter.25.cloned.1.call-start = ((), (), s32[]{:S(2)}) async-start(), calls=%async_computation.26 | async-start | bytes 5013504 | tf_op jit(solution)/shard_map/reduce_scatter | solution.py:216
  786.9 3.4 copy-start.3
  790.4 163.0 %all-gather.17.cloned.1.call-start = ((), (), s32[]{:S(2)}) async-start(), calls=%async_computation.28 | async-start | bytes 4259840 | tf_op jit(solution)/shard_map/all_gather | solution.py:39
  887.2 151.9 %all-gather.13.cloned.1.call-start = ((), (), s32[]{:S(2)}) async-start(), calls=%async_computation.20 | async-start | bytes 5570560 | tf_op jit(solution)/shard_map/all_gather | solution.py:39
  890.8 169.3 %reduce-scatter.29.cloned.1.call-start = ((), (), s32[]{:S(2)}) async-start(), calls=%async_computation.29 | async-start | bytes 1671168 | tf_op jit(solution)/shard_map/reduce_scatter | solution.py:49
  957.8 86.5 %copy-start.12 = (bf16[1024,272]{0,1:T(8,128)(2,1)S(1)}, bf16[1024,272]{0,1:T(8,128)(2,1)}, u32[]{:S(2)}) copy-start(bf16[1024,272]{0,1:T(8,128)(2,1)} %copy-done.11) | copy-start | bytes 1671172
  957.8 112.9 %reduce-scatter.17.cloned.1.call-start = ((), (), s32[]{:S(2)}) async-start(), calls=%async_computation.21 | async-start | bytes 1671168 | tf_op jit(solution)/shard_map/reduce_scatter | solution.py:49
  1044.2 5.6 copy-start.14
  1044.2 178.8 %all-reduce.6.cloned.1.call-start = ((), (), s32[]{:S(2)}) async-start(), calls=%async_computation.30 | async-start | bytes 14483456 | tf_op jit(solution)/shard_map/psum | solution.py:239
  1049.9 5.3 copy-start.6
  1049.9 6.8 copy-start.25
  1059.0 1.1 copy-start.20
  1059.1 11.6 copy-start.5
  1059.1 11.6 copy-start.8
  1059.1 11.6 copy-start.22
  1223.1 3.0 copy-start.17
  1223.1 3.8 copy-start.10
  1226.9 2.5 copy-start.9
  1226.9 3.9 copy-start.1
Sparse Core Ops, SparseCore 0:
  40.6 116.7 reduce-scatter.10
  164.6 32.3 all-gather.8
  199.1 30.7 all-gather.6
  241.0 30.0 all-gather.10
  274.0 6.9 reduce-scatter.12
  283.3 154.3 reduce-scatter.18
  440.2 153.3 reduce-scatter.14
  601.8 85.9 all-gather.14
  692.7 7.0 reduce-scatter.20
  719.0 44.1 reduce-scatter.22
  775.7 51.8 reduce-scatter.26
  829.7 50.5 reduce-scatter.24
  887.3 65.9 all-gather.16
  955.4 83.7 all-gather.12
  1041.2 7.0 reduce-scatter.28
  1050.6 9.7 reduce-scatter.16
  1065.2 157.8 all-reduce.5
where the time goes:
time: 1240 us
  waiting for transfers between devices  954 us (77%)
  blocking collectives  130 us (10%)
  matrix products  82.7 us (7%)
  other arithmetic  35.4 us (3%)
  local copies, waits for them, and re-layouts  19.8 us (2%)
  between operations  14.4 us (1%)
    reduce_scatter x4, waiting for transfers between devices, width_product(): lax.psum_scatter(contract(left_side, weight, flipped), 'row', scatter_dim...  441 us
    all_gather x4, waiting for transfers between devices, gather_rows(): return lax.all_gather(values, 'row', axis=0, tiled=True)  260 us
    psum x1, waiting for transfers between devices, shards(): lax.psum((qkv_weight_grad, output_weight_grad, up_weight_grad, down_weigh...  106 us
    reduce_scatter x1, waiting for transfers between devices, shards(): lax.psum_scatter(key_part.reshape(group_rows, D), ('row', 'col'), scatter...  51.5 us
    psum x1, blocking collectives, shards(): lax.psum((stacked, widen(up_bias_part, FF, col_index)), ('dp', 'row', 'co...  41.8 us
    psum x4, blocking collectives, row_single(): return lax.psum(values, 'row')  41.5 us
    reduce_scatter x1, waiting for transfers between devices, shards(): lax.psum_scatter(value_part.reshape(group_rows, D), ('row', 'col'), scatt...  32.2 us
    all_gather x1, waiting for transfers between devices, shards(): lax.all_gather(heads_in[:, D:2 * D], ('row', 'col'), axis=0, tiled=True)  31.2 us
  transfers between devices with their start and end apart: 17, of which 14 were waited for; matrix products, arithmetic and copies ran while one was open for 6% of the time, Pallas kernels for 0%

commit v1 on v0

v1 whole, which is shorter than its diff:
```python
import jax
import jax.numpy as jnp
from jax import lax
from jax.sharding import PartitionSpec as P

D = 1088
HEADS = 17
HEAD_DIM = 64
FF = 4352
epsilon = 1e-05
f32 = jnp.float32
bf16 = jnp.bfloat16


def gelu_exact(before):
    return jax.nn.gelu(before, approximate=False)


def dot(left, right, left_dim, right_dim):
    return lax.dot_general(
        left, right, (((left_dim,), (right_dim,)), ((), ())), preferred_element_type=f32
    )


def swap(values, axis, k):
    return lax.ppermute(values, axis, [(i, i ^ k) for i in range(lax.axis_size(axis))])


def spread(values, axis):
    return [values] + [swap(values, axis, k) for k in range(1, lax.axis_size(axis))]


def trade(pieces, axis):
    return [pieces[0]] + [swap(pieces[k], axis, k) for k in range(1, len(pieces))]


def settle(pieces, index):
    pieces = list(pieces)
    bit = 1
    while bit < len(pieces):
        odd = (index & bit) != 0
        pieces = [jnp.where(odd, pieces[k ^ bit], pieces[k]) for k in range(len(pieces))]
        bit *= 2
    return pieces


def total(pieces):
    out = pieces[0].astype(f32)
    for piece in pieces[1:]:
        out = out + piece.astype(f32)
    return out


def cut(values, start, size, dim):
    return lax.dynamic_slice_in_dim(values, start, size, dim)


def norm_forward(rows, gain, shift):
    average = jnp.sum(rows, 0, keepdims=True) / D
    centered = rows - average
    variance = jnp.sum(centered * centered, 0, keepdims=True) / D
    inverse = lax.rsqrt(variance + epsilon)
    normal = centered * inverse
    return (normal * gain + shift).astype(bf16), normal, inverse


def norm_backward(upstream, normal, inverse, gain):
    scaled = upstream * gain
    first = jnp.sum(scaled, 0, keepdims=True) / D
    second = jnp.sum(scaled * normal, 0, keepdims=True) / D
    return inverse * (scaled - first - normal * second)


def attend(queries, keys, values, allowed):
    scores = jnp.einsum("hdk,hdq->hkq", keys, queries, preferred_element_type=f32)
    scores = jnp.where(allowed[None], scores * HEAD_DIM ** (-0.5), -1e30)
    powers = jnp.exp(scores - jnp.max(scores, 1, keepdims=True))
    probability = powers / jnp.sum(powers, 1, keepdims=True)
    out = jnp.einsum(
        "hdk,hkq->hdq", values, probability.astype(bf16), preferred_element_type=f32
    ).astype(bf16)
    return probability, out


def attend_back(queries, keys, values, probability, grad_out):
    scale = HEAD_DIM ** (-0.5)
    grad_weights = jnp.einsum("hdk,hdq->hkq", values, grad_out, preferred_element_type=f32)
    inner = jnp.sum(probability * grad_weights, 1, keepdims=True)
    grad_scores = (probability * (grad_weights - inner)).astype(bf16)
    grad_q = jnp.einsum("hdk,hkq->hdq", keys, grad_scores, preferred_element_type=f32) * scale
    grad_k = jnp.einsum("hdq,hkq->hdk", queries, grad_scores, preferred_element_type=f32) * scale
    grad_v = jnp.einsum(
        "hdq,hkq->hdk", grad_out, probability.astype(bf16), preferred_element_type=f32
    )
    return grad_q, grad_k, grad_v


def shards(
    tokens,
    block_order,
    first_gain,
    first_shift,
    qkv_weight,
    query_value_bias,
    output_weight,
    output_bias,
    second_gain,
    second_shift,
    up_weight,
    up_bias,
    down_weight,
    down_bias,
    cotangent,
):
    R, G = lax.axis_size("row"), lax.axis_size("dp")
    r, c, g = lax.axis_index("row"), lax.axis_index("col"), lax.axis_index("dp")
    low = c == 0
    db, T = tokens.shape
    tq = T // R
    hp = HEADS // R
    W = hp * HEAD_DIM
    E = HEADS * HEAD_DIM - W * R
    X = E // HEAD_DIM
    half = W // 2
    pw = max(half, 2 * E)
    sub = up_weight.shape[1] // R
    GH = G // 2
    hr = db // GH

    def pad(values):
        return jnp.pad(values, ((0, 0), (0, pw - values.shape[1])))

    x = jnp.concatenate(spread(tokens, "row"), 0).astype(f32)
    vectors = jnp.concatenate(
        spread(
            jnp.stack([first_gain, first_shift, output_bias, second_gain, second_shift]), "row"
        ),
        1,
    )
    g1, s1, ob, g2, s2 = [vectors[i][:, None] for i in range(5)]

    side = qkv_weight.shape[1] - D
    own_part = cut(qkv_weight, c * side, D, 1)
    own_keys = cut(qkv_weight, (1 - c) * D, side, 1)
    other_keys = swap(own_keys, "col", 1)
    key_part = jnp.concatenate(
        [jnp.where(low, own_keys, other_keys), jnp.where(low, other_keys, own_keys)], 1
    )
    source = jnp.where(g == 3, key_part, own_part)
    extras = pad(jnp.concatenate([own_part[:, R * W :], key_part[:, R * W :]], 1))
    offset = jnp.where(g == 3, c, g & 1) * half
    chunks = [
        jnp.where(g == 2, extras, pad(cut(source, (r ^ k) * W + offset, half, 1)))
        for k in range(R)
    ]
    piece = jnp.concatenate(trade(chunks, "row"), 0)
    own_w = jnp.concatenate(settle(spread(piece, "dp"), g), 1)
    other_w = swap(own_w, "col", 1)
    lo, hi = jnp.where(low, own_w, other_w), jnp.where(low, other_w, own_w)
    ex = 2 * pw
    kk = 3 * pw
    wqkv = jnp.concatenate(
        [
            lo[:, :half],
            lo[:, pw : pw + half],
            lo[:, ex : ex + E],
            lo[:, kk : kk + half],
            hi[:, kk : kk + half],
            lo[:, ex + E : ex + 2 * E],
            hi[:, :half],
            hi[:, pw : pw + half],
            hi[:, ex : ex + E],
        ],
        1,
    )
    HW = W + E
    bias = jnp.concatenate(
        [
            cut(query_value_bias[0], r * W, W, 0),
            query_value_bias[0, R * W :],
            jnp.zeros((HW,), f32),
            cut(query_value_bias[1], r * W, W, 0),
            query_value_bias[1, R * W :],
        ]
    )[:, None]

    part = cut(output_weight, g * (output_weight.shape[0] // G), output_weight.shape[0] // G, 0)
    part = jnp.concatenate(spread(part, "row"), 1)
    own_o = jnp.concatenate(settle(spread(part, "dp"), g), 0)
    other_o = swap(own_o, "col", 1)
    wo = jnp.concatenate([jnp.where(low, own_o, other_o), jnp.where(low, other_o, own_o)], 0)

    part = jnp.where(
        g < GH,
        cut(up_weight, (g % GH) * hr, hr, 0),
        cut(down_weight, (g % GH) * hr, hr, 0),
    )
    part = jnp.stack(trade([cut(part, (r ^ k) * sub, sub, 1) for k in range(R)], "row"))
    own_f = settle(spread(part, "dp"), g)
    own_f = jnp.stack(
        [
            jnp.stack(own_f[:GH], 1).reshape(D, sub),
            jnp.stack(own_f[GH:], 1).reshape(D, sub),
        ]
    )
    wf = jnp.concatenate([own_f, swap(own_f, "col", 1)], 2)
    wup, wdn = wf[0], wf[1]
    own_ub = cut(up_bias, r * sub, sub, 0)
    ub = jnp.concatenate([own_ub, swap(own_ub, "col", 1)])[:, None]

    block = T * 2 // block_order.shape[1]
    places = (
        block_order.reshape(-1)[:, None] * block + jnp.arange(block, dtype=jnp.int32)[None, :]
    ).reshape(-1)
    own_places = cut(places, c * T, T, 0)
    key_places = jnp.concatenate([own_places, cut(places, (1 - c) * T, T, 0)])
    allowed = key_places[:, None] <= own_places[None, :]
    extra_allowed = cut(allowed, r * tq, tq, 1)

    normed1, n1, inv1 = norm_forward(x, g1, s1)
    projected = (dot(wqkv, normed1, 0, 0) + bias).astype(bf16)
    own_kv = projected[HW:]
    kv = jnp.concatenate([own_kv, swap(own_kv, "col", 1)], 1)
    S = 2 * T
    queries = projected[:W].reshape(hp, HEAD_DIM, T)
    keys = kv[:W].reshape(hp, HEAD_DIM, S)
    values = kv[HW : HW + W].reshape(hp, HEAD_DIM, S)
    qx = cut(projected[W:HW], r * tq, tq, 1).reshape(X, HEAD_DIM, tq)
    kx = kv[W:HW].reshape(X, HEAD_DIM, S)
    vx = kv[HW + W :].reshape(X, HEAD_DIM, S)
    prob, out = attend(queries, keys, values, allowed)
    probx, outx = attend(qx, kx, vx, extra_allowed)
    packed = jnp.concatenate([out.reshape(W, T), outx.reshape(E // R, T)], 0)
    rows = settle(spread(packed, "row"), r)
    attended = jnp.concatenate(
        [piece[:W] for piece in rows]
        + [jnp.concatenate([piece[W:].reshape(E, tq) for piece in rows], 1)],
        0,
    )
    middle = x + dot(wo, attended, 0, 0) + ob
    normed2, n2, inv2 = norm_forward(middle, g2, s2)

    before = dot(wup, normed2, 0, 0) + ub
    hidden = gelu_exact(before).astype(bf16)
    down = dot(wdn, hidden, 1, 0)
    down = total([down[:db]] + trade(list(down.astype(bf16).reshape(R, db, T)), "row")[1:])
    result = (middle[:db] + down + down_bias[:, None]).astype(bf16)

    upstream = jnp.concatenate(spread(cotangent, "row"), 0)
    grad_hidden = dot(wdn, upstream, 0, 0)
    grad_before = jax.vjp(gelu_exact, before)[1](grad_hidden)[0].astype(bf16)
    part2 = dot(wup, grad_before, 1, 0)
    sg_part = jnp.sum(part2 * n2, 1)
    ss_part = jnp.sum(part2, 1)
    back2 = norm_backward(part2, n2, inv2, g2)
    back2_low = back2.astype(bf16)
    arrived = trade([cut(back2_low, (r ^ k) * tq, tq, 1) for k in range(R)], "row")
    mine = cut(back2, r * tq, tq, 1) + cut(upstream, r * tq, tq, 1).astype(f32)
    for k in range(1, R):
        blocks = arrived[k].reshape(R, db, tq)
        mine = mine + jnp.concatenate([blocks[j ^ k] for j in range(R)], 0).astype(f32)
    branch = mine.astype(bf16)
    ob_part = jnp.sum(branch.astype(f32), 1)
    grad_att = dot(wo, branch, 1, 0).astype(bf16)
    go = jnp.concatenate(
        settle(trade([cut(grad_att, (r ^ k) * W, W, 0) for k in range(R)], "row"), r), 1
    ).reshape(hp, HEAD_DIM, T)
    gox = grad_att[R * W :].reshape(X, HEAD_DIM, tq)
    branch_rows = jnp.concatenate(
        settle(trade(list(branch.reshape(R, db, tq)), "row"), r), 1
    )

    dw_down = dot(upstream, hidden, 1, 1)
    dw_up = dot(normed2, grad_before, 1, 1)
    away = jnp.stack([dw_up[:, sub:], dw_down[:, sub:]]).astype(bf16)
    home = jnp.stack([dw_up[:, :sub], dw_down[:, :sub]])
    both = (home + swap(away, "col", 1).astype(f32)).astype(bf16)
    both = both.reshape(2, R, GH, hr, sub).transpose(0, 2, 1, 3, 4).reshape(G, R, hr, sub)
    both = total(
        trade([lax.dynamic_index_in_dim(both, g ^ k, 0, False) for k in range(G)], "dp")
    ).astype(bf16)
    both = jnp.concatenate(settle(trade(list(both), "row"), r), 1)
    both = settle(spread(both, "dp"), g)
    up_weight_grad = jnp.concatenate(both[:GH], 0).astype(f32)
    down_weight_grad = jnp.concatenate(both[GH:], 0).astype(f32)

    dwo = dot(attended, branch_rows, 1, 1)
    side_rows = dwo.shape[0] // 2
    lo_o, hi_o = dwo[:side_rows], dwo[side_rows:]
    arrived = swap(jnp.where(low, hi_o, lo_o).astype(bf16), "col", 1)
    mine_o = (jnp.where(low, lo_o, hi_o) + arrived.astype(f32)).astype(bf16)
    mine_o = mine_o.reshape(G, side_rows // G, db)
    mine_o = total(
        trade([lax.dynamic_index_in_dim(mine_o, g ^ k, 0, False) for k in range(G)], "dp")
    ).astype(bf16)
    output_weight_grad = jnp.concatenate(settle(spread(mine_o, "dp"), g), 0).astype(f32)

    gq, gk, gv = attend_back(queries, keys, values, prob, go)
    gqx, gkx, gvx = attend_back(qx, kx, vx, probx, gox)
    gkv = jnp.concatenate(
        [gk.reshape(W, S), gkx.reshape(E, S), gv.reshape(W, S), gvx.reshape(E, S)], 0
    )
    gkv = (gkv[:, :T] + swap(gkv[:, T:].astype(bf16), "col", 1).astype(f32)).astype(bf16)
    gqx = lax.dynamic_update_slice_in_dim(
        jnp.zeros((E, T), bf16), gqx.reshape(E, tq).astype(bf16), r * tq, 1
    )
    grad_p = jnp.concatenate([gq.reshape(W, T).astype(bf16), gqx, gkv], 0)
    sums = jnp.sum(grad_p.astype(f32), 1)
    part1 = dot(wqkv, grad_p, 1, 0)
    fg_part = jnp.sum(part1 * n1, 1)
    fs_part = jnp.sum(part1, 1)
    back1 = norm_backward(part1, n1, inv1, g1)
    back1 = total([back1[:db]] + trade(list(back1.astype(bf16).reshape(R, db, T)), "row")[1:])
    input_grad = branch_rows.astype(f32) + back1

    dw = dot(normed1, grad_p, 1, 1)
    dq, dqx, dk, dkx, dv, dvx = jnp.split(
        dw, [W, HW, HW + W, 2 * HW, 2 * HW + W], 1
    )

    def grid(main, main_x, main_k):
        return jnp.concatenate(
            [
                pad(main[:, :half]),
                pad(main[:, half:]),
                pad(jnp.concatenate([main_x, dkx], 1)),
                pad(main_k),
            ],
            1,
        )

    lo_w, hi_w = grid(dq, dqx, dk[:, :half]), grid(dv, dvx, dk[:, half:])
    arrived = swap(jnp.where(low, hi_w, lo_w).astype(bf16), "col", 1)
    mine_w = (jnp.where(low, lo_w, hi_w) + arrived.astype(f32)).astype(bf16)
    mine_w = total(
        trade([cut(mine_w, (g ^ k) * pw, pw, 1) for k in range(G)], "dp")
    ).astype(bf16)
    mine_w = jnp.stack(settle(trade(list(mine_w.reshape(R, db, pw)), "row"), r))
    parts = settle(spread(mine_w, "dp"), g)
    ends = total([parts[2][i] for i in range(R)])
    mains = [p[:, :half].astype(f32) for i in range(R) for p in (parts[0][i], parts[1][i])]
    keys_own = jnp.stack([parts[3][i][:, :half] for i in range(R)])
    keys_other = swap(keys_own, "col", 1)
    keys_lo = jnp.where(low, keys_own, keys_other).astype(f32)
    keys_hi = jnp.where(low, keys_other, keys_own).astype(f32)
    keys_grad = jnp.concatenate(
        [p for i in range(R) for p in (keys_lo[i], keys_hi[i])] + [ends[:, E : 2 * E]], 1
    )
    main_grad = jnp.concatenate(mains + [ends[:, :E]], 1)
    qkv_weight_grad = jnp.where(
        low,
        jnp.concatenate([main_grad, keys_grad[:, :side]], 1),
        jnp.concatenate([keys_grad[:, D - side :], main_grad], 1),
    )

    rel = jnp.stack([fg_part, fs_part, ob_part, sg_part, ss_part])
    rel = jnp.concatenate(settle(jnp.split(rel, R, 1), r), 1)

    def widen(values, width, start):
        return lax.dynamic_update_slice_in_dim(jnp.zeros((width,), f32), values, start, 0)

    db_part = widen(jnp.sum(cotangent.astype(f32), 1), D, r * db)

    def placed(values):
        return jnp.concatenate([widen(values[:W], R * W, r * W), values[W:]])

    ub_sum = jnp.sum(grad_before.astype(f32), 1)
    full = up_bias.shape[0]
    ub_part = widen(ub_sum[:sub], 2 * full, c * full + r * sub) + widen(
        ub_sum[sub:], 2 * full, (1 - c) * full + r * sub
    )
    small = jnp.concatenate(
        [
            rel,
            db_part[None],
            placed(sums[:HW])[None],
            placed(sums[2 * HW :])[None],
            ub_part.reshape(-1, D),
        ],
        0,
    )
    for axis in ("col", "row", "dp"):
        k = 1
        while k < lax.axis_size(axis):
            small = small + swap(small, axis, k)
            k *= 2
    return (
        result,
        input_grad,
        small[0],
        small[1],
        qkv_weight_grad,
        small[6:8],
        output_weight_grad,
        small[2],
        small[3],
        small[4],
        up_weight_grad,
        small[8:].reshape(-1),
        down_weight_grad,
        small[5],
    )


def solution(mesh):
    placed = (
        P("row", ("dp", "col")),
        P("dp", None),
        P("row"),
        P("row"),
        P("row", "col"),
        P(),
        P("col", "row"),
        P("row"),
        P("row"),
        P("row"),
        P("row", "col"),
        P("col"),
        P("row", "col"),
        P("row"),
        P("row", ("dp", "col")),
    )
    return jax.shard_map(
        shards,
        mesh=mesh,
        in_specs=placed,
        out_specs=(
            P("row", ("dp", "col")),
            P("row", ("dp", "col")),
            P(),
            P(),
            P("row", "col"),
            P(),
            P("col", "row"),
            P(),
            P(),
            P(),
            P("row", "col"),
            P(),
            P("row", "col"),
            P(),
        ),
        check_vma=False,
    )
```

time: 1240 us -> 529 us (0.43)
  waiting for transfers between devices: 954 us -> 210 us
  blocking collectives: 130 us -> 0 us
  starting transfers between devices: 0.92 us -> 101 us
  local copies, waits for them, and re-layouts: 19.8 us -> 80.2 us
  other arithmetic: 35.4 us -> 68.3 us
  matrix products: 82.7 us -> 57.1 us
    reduce_scatter x10 -> x0, waiting for transfers between devices: 532 us -> none  [the longest x4 441 us: width_product(): lax.psum_scatter(contract(left_side, weight, flipped), 'row', scatter_dim...]
    all_gather x6 -> x0, waiting for transfers between devices: 315 us -> none  [the longest x4 260 us: gather_rows(): return lax.all_gather(values, 'row', axis=0, tiled=True)]
    ppermute x0 -> x85, waiting for transfers between devices: none -> 210 us  [swap(): lax.ppermute(values, axis, [(i, i ^ k) for i in range(lax.axis_size(axis))])]
    psum x1 -> x0, waiting for transfers between devices: 106 us -> none  [shards(): lax.psum((qkv_weight_grad, output_weight_grad, up_weight_grad, down_weigh...]
    psum x7 -> x0, blocking collectives: 104 us -> none  [the longest x1 41.8 us: shards(): lax.psum((stacked, widen(up_bias_part, FF, col_index)), ('dp', 'row', 'co...]
    ppermute x0 -> x85, starting transfers between devices: none -> 101 us  [swap(): lax.ppermute(values, axis, [(i, i ^ k) for i in range(lax.axis_size(axis))])]
    dot_general x18 -> x23, matrix products: 82.7 us -> 49.3 us  [the longest x12 31.7 us: dot(): lax.dot_general(left, right, (((left_dim,), (right_dim,)), ((), ())), pre...]
    another operation x16 -> x28, local copies, waits for them, and re-layouts: 0.2 us -> 16.9 us  [the longest x1 4.74 us: shards(): jnp.stack([jnp.stack(own_f[:GH], 1).reshape(D, sub), jnp.stack(own_f[GH:]...]
  transfers between devices with their start and end apart: 17 -> 85, of which waited for: 14 -> 34; matrix products, arithmetic and copies ran while one was open for 6% -> 30% of each run, Pallas kernels for 0% -> 0%
where the time goes in v1:
time: 529 us; the launch traced here: 520 us
  waiting for transfers between devices  210 us (40%)
  starting transfers between devices  101 us (19%)
  local copies, waits for them, and re-layouts  80.2 us (15%)
  other arithmetic  68.3 us (13%)
  matrix products  57.1 us (11%)
    ppermute x85, waiting for transfers between devices, swap(): lax.ppermute(values, axis, [(i, i ^ k) for i in range(lax.axis_size(axis))])  210 us
    ppermute x85, starting transfers between devices, swap(): lax.ppermute(values, axis, [(i, i ^ k) for i in range(lax.axis_size(axis))])  101 us
    dot_general x12, matrix products, dot(): lax.dot_general(left, right, (((left_dim,), (right_dim,)), ((), ())), pre...  31.7 us
    unnamed x251, local copies, waits for them, and re-layouts  13.2 us
  transfers between devices with their start and end apart: 85, of which 34 were waited for; matrix products, arithmetic and copies ran while one was open for 30% of the time, Pallas kernels for 0%

profile of v1, /device:TPU:0, one launch (start us, length us, event | category | flops | bytes accessed | tf_op | source)
XLA Modules:
  0.0 519.8 jit_solution(8779076885398104629)
XLA Ops:
  4.2 5.1 collective-permute-start.20
  24.4 2.3 collective-permute-done.18
  26.8 2.6 collective-permute-start.1
  29.4 8.3 %collective-permute-done.4 = bf16[136,272]{1,0:T(8,128)(2,1)} collective-permute-done((bf16[136,272]{1,0:T(8,128)(2,1)}, bf16[136,272]{1,0:T(8,128)(2,1)}, u32[]{:S(2)}, u32[]{:S(2)}) %collective-permute-start.4) | collective-permute-done | bytes 74016 | tf_op jit(solution)/shard_map/ppermute | solution.py:26
  37.7 2.4 collective-permute-start.2
  48.5 14.8 %collective-permute-done.26 = bf16[136,544]{1,0:T(8,128)(2,1)} collective-permute-done((bf16[136,544]{1,0:T(8,128)(2,1)}, bf16[136,544]{1,0:T(8,128)(2,1)}, u32[]{:S(2)}, u32[]{:S(2)}) %collective-permute-start.26) | collective-permute-done | bytes 148000 | tf_op jit(solution)/shard_map/ppermute | solution.py:26
  63.4 2.5 collective-permute-start.38
  70.8 13.6 %collective-permute-done.36 = bf16[272,512]{1,0:T(8,128)(2,1)S(1)} collective-permute-done((bf16[272,512]{1,0:T(8,128)(2,1)}, bf16[272,512]{1,0:T(8,128)(2,1)S(1)}, u32[]{:S(2)}, u32[]{:S(2)}) %collective-permute-start.36) | collective-permute-done | bytes 278560 | tf_op jit(solution)/shard_map/ppermute | solution.py:26
  86.0 2.4 collective-permute-start.11
  92.5 3.4 collective-permute-done.12
  100.2 5.4 %collective-permute-done.16 = bf16[1088,128]{1,0:T(8,128)(2,1)S(1)} collective-permute-done((bf16[1088,128]{1,0:T(8,128)(2,1)S(1)}, bf16[1088,128]{1,0:T(8,128)(2,1)S(1)}, u32[]{:S(2)}, u32[]{:S(2)}) %collective-permute-start.16) | collective-permute-done | bytes 278560 | tf_op jit(solution)/shard_map/ppermute | solution.py:26
  105.6 2.4 collective-permute-start.6
  108.1 9.7 %collective-permute-done.15 = bf16[1088,128]{1,0:T(8,128)(2,1)S(1)} collective-permute-done((bf16[1088,128]{1,0:T(8,128)(2,1)S(1)}, bf16[1088,128]{1,0:T(8,128)(2,1)S(1)}, u32[]{:S(2)}, u32[]{:S(2)}) %collective-permute-start.15) | collective-permute-done | bytes 278560 | tf_op jit(solution)/shard_map/ppermute | solution.py:26
  123.9 12.5 %collective-permute-done.30 = bf16[4,136,544]{2,1,0:T(8,128)(2,1)S(1)} collective-permute-done((bf16[4,136,544]{2,1,0:T(8,128)(2,1)S(1)}, bf16[4,136,544]{2,1,0:T(8,128)(2,1)S(1)}, u32[]{:S(2)}, u32[]{:S(2)}) %collective-permute-start.30) | collective-permute-done | bytes 591904 | tf_op jit(solution)/shard_map/ppermute | solution.py:26
  136.3 12.0 %collective-permute-done.29 = bf16[4,136,544]{2,1,0:T(8,128)(2,1)S(1)} collective-permute-done((bf16[4,136,544]{2,1,0:T(8,128)(2,1)S(1)}, bf16[4,136,544]{2,1,0:T(8,128)(2,1)S(1)}, u32[]{:S(2)}, u32[]{:S(2)}) %collective-permute-start.29) | collective-permute-done | bytes 591904 | tf_op jit(solution)/shard_map/ppermute | solution.py:26
  150.0 2.9 select_bitcast_fusion.3
  156.2 4.4 concatenate.140
  160.7 3.3 add_convert_fusion.3
  167.4 2.0 pad_maximum_fusion.3
  169.4 4.7 copy.60
  182.0 2.1 fusion.61
  184.1 7.9 %fusion.128 = (f32[4,512]{1,0:T(4,128)S(1)}, f32[4,1024,512]{2,1,0:T(8,128)}) fusion(pred[1024,512]{1,0:T(8,128)(4,1)} %broadcast_compare_fusion, bf16[4,64,1024]{2,1,0:T(8,128)(2,1)} %bitcast.224, bf16[4,64,512]{2,1,0:T(8,128)(2,1)} %bitcast.237), kind=kOutput, calls=%fused_computation.406 | convolution fusion | flops 276825088 | bytes 9707520 | tf_op jit(solution)/shard_map/sub | solution.py:77
  192.0 4.5 fusion.44
  201.0 3.2 broadcast_select_fusion.1
  204.2 6.1 %collective-permute-done.24 = bf16[272,512]{1,0:T(8,128)(2,1)S(1)} collective-permute-done((bf16[272,512]{1,0:T(8,128)(2,1)S(1)}, bf16[272,512]{1,0:T(8,128)(2,1)S(1)}, u32[]{:S(2)}, u32[]{:S(2)}) %collective-permute-start.24) | collective-permute-done | bytes 278560 | tf_op jit(solution)/shard_map/ppermute | solution.py:26
  210.3 9.6 %collective-permute-done.23 = bf16[272,512]{1,0:T(8,128)(2,1)S(1)} collective-permute-done((bf16[272,512]{1,0:T(8,128)(2,1)S(1)}, bf16[272,512]{1,0:T(8,128)(2,1)S(1)}, u32[]{:S(2)}, u32[]{:S(2)}) %collective-permute-start.23) | collective-permute-done | bytes 278560 | tf_op jit(solution)/shard_map/ppermute | solution.py:26
  230.2 3.7 fusion.129
  235.7 4.5 copy.61
  240.2 4.6 pad_maximum_fusion
  244.8 6.3 %multiply_convert_fusion.1 = (bf16[1088,512]{1,0:T(8,128)(2,1)S(1)}, f32[1088,512]{1,0:T(8,128)S(1)}, f32[1088,512]{1,0:T(8,128)S(1)}) fusion(f32[1088]{0:T(1024)S(1)} %copy-done.101, f32[1088,512]{1,0:T(8,128)S(1)} %copy-done.5, f32[1088]{0:T(1024)S(1)} %copy-done.105, f32[1088]{0:T(1024)S(1)} %copy-done.81, f32[512]{0:T(512)S(1)} %add_rsqrt_fusion, ...), kind=kOutput, calls=%fused_computation.54 | convolution fusion | flops 1251704832 | bytes 10334208 | tf_op jit(solution)/shard_map/dot_general | solution.py:20
  251.2 2.5 convert_reduce_fusion.1
  253.7 2.7 multiply_reduce_fusion.1
  260.0 3.2 fusion.130
  270.0 5.2 %collective-permute-start.39 = (bf16[1088,128]{1,0:T(8,128)(2,1)}, bf16[1088,128]{1,0:T(8,128)(2,1)}, u32[]{:S(2)}, u32[]{:S(2)}) collective-permute-start(bf16[1088,128]{1,0:T(8,128)(2,1)} %get-tuple-element.122), channel_id=1, source_target_pairs={{0,2},{2,0},{4,6},{6,4},{1,3},{3,1},{5,7},{7,5},{8,10},{10,8},{12,... | collective-permute-start | bytes 835592 | tf_op jit(solution)/shard_map/ppermute | solution.py:26
  275.3 2.5 collective-permute-start.41
  287.2 4.4 collective-permute-done.41
  292.6 25.9 %collective-permute-done.40 = bf16[1088,128]{1,0:T(8,128)(2,1)S(1)} collective-permute-done((bf16[1088,128]{1,0:T(8,128)(2,1)S(1)}, bf16[1088,128]{1,0:T(8,128)(2,1)S(1)}, u32[]{:S(2)}, u32[]{:S(2)}) %collective-permute-start.40) | collective-permute-done | bytes 278560 | tf_op jit(solution)/shard_map/ppermute | solution.py:26
  324.1 2.0 collective-permute-start.46
  326.1 2.3 collective-permute-start.45
  328.5 2.2 fusion.59
  331.3 2.1 collective-permute-start.43
  333.3 2.3 collective-permute-start.42
  337.4 2.4 multiply_convert_fusion
  339.8 2.4 fusion.33
  343.2 2.3 convolution_multiply_fusion
  352.5 2.0 collective-permute-done.71
  361.4 2.3 collective-permute-done.73
  372.6 3.7 fusion.18
  382.4 4.3 collective-permute-done.53
  387.0 5.4 %collective-permute-done.54 = f32[12,1088]{1,0:T(8,128)S(1)} collective-permute-done((f32[12,1088]{1,0:T(8,128)S(1)}, f32[12,1088]{1,0:T(8,128)S(1)}, u32[]{:S(2)}, u32[]{:S(2)}) %collective-permute-start.54) | collective-permute-done | bytes 52256 | tf_op jit(solution)/shard_map/ppermute | solution.py:26
  393.5 2.0 fusion.111
  405.4 2.7 collective-permute-done.58
  416.6 2.9 collective-permute-done.51
  421.0 12.7 %collective-permute-done.50 = bf16[272,512]{1,0:T(8,128)(2,1)S(1)} collective-permute-done((bf16[272,512]{1,0:T(8,128)(2,1)S(1)}, bf16[272,512]{1,0:T(8,128)(2,1)S(1)}, u32[]{:S(2)}, u32[]{:S(2)}) %collective-permute-start.50) | collective-permute-done | bytes 278560 | tf_op jit(solution)/shard_map/ppermute | solution.py:26
  433.7 2.1 fusion.54
  440.1 3.8 fusion.2
  443.9 4.3 copy.68
  456.2 11.1 %collective-permute-done.76 = bf16[4,136,544]{2,1,0:T(8,128)(2,1)S(1)} collective-permute-done((bf16[4,136,544]{2,1,0:T(8,128)(2,1)S(1)}, bf16[4,136,544]{2,1,0:T(8,128)(2,1)S(1)}, u32[]{:S(2)}, u32[]{:S(2)}) %collective-permute-start.76) | collective-permute-done | bytes 591904 | tf_op jit(solution)/shard_map/ppermute | solution.py:26
  467.3 9.6 %collective-permute-done.78 = bf16[4,136,544]{2,1,0:T(8,128)(2,1)S(1)} collective-permute-done((bf16[4,136,544]{2,1,0:T(8,128)(2,1)S(1)}, bf16[4,136,544]{2,1,0:T(8,128)(2,1)S(1)}, u32[]{:S(2)}, u32[]{:S(2)}) %collective-permute-start.78) | collective-permute-done | bytes 591904 | tf_op jit(solution)/shard_map/ppermute | solution.py:26
  480.3 2.7 collective-permute-start.79
  486.8 2.6 concatenate.167
  489.3 2.5 collective-permute-done.80
  500.2 9.2 %collective-permute-done.84 = bf16[136,2176]{1,0:T(8,128)(2,1)S(1)} collective-permute-done((bf16[136,2176]{1,0:T(8,128)(2,1)S(1)}, bf16[136,2176]{1,0:T(8,128)(2,1)S(1)}, u32[]{:S(2)}, u32[]{:S(2)}) %collective-permute-start.84) | collective-permute-done | bytes 591904 | tf_op jit(solution)/shard_map/ppermute | solution.py:26
  509.4 6.9 %collective-permute-done.83 = bf16[136,2176]{1,0:T(8,128)(2,1)S(1)} collective-permute-done((bf16[136,2176]{1,0:T(8,128)(2,1)S(1)}, bf16[136,2176]{1,0:T(8,128)(2,1)S(1)}, u32[]{:S(2)}, u32[]{:S(2)}) %collective-permute-start.83) | collective-permute-done | bytes 591904 | tf_op jit(solution)/shard_map/ppermute | solution.py:26
  (572 shorter events, 190.0 us)
Async XLA Ops:
  4.2 17.0 %collective-permute-start.20 = (f32[5,272]{1,0:T(8,128)S(1)}, f32[5,272]{1,0:T(8,128)S(1)}, u32[]{:S(2)}, u32[]{:S(2)}) collective-permute-start(f32[5,272]{1,0:T(8,128)S(1)} %stack.115), channel_id=1, source_target_pairs={{0,6},{2,4},{4,2},{6,0},{1,7},{3,5},{5,3},{7,1},{8,14},{10,12},{12... | collective-permute-start | bytes 16328 | tf_op jit(solution)/shard_map/ppermute | solution.py:26
  9.3 13.4 %collective-permute-start.19 = (f32[5,272]{1,0:T(8,128)S(1)}, f32[5,272]{1,0:T(8,128)S(1)}, u32[]{:S(2)}, u32[]{:S(2)}) collective-permute-start(f32[5,272]{1,0:T(8,128)S(1)} %stack.115), channel_id=1, source_target_pairs={{0,4},{2,6},{4,0},{6,2},{1,5},{3,7},{5,1},{7,3},{8,12},{10,14},{12... | collective-permute-start | bytes 16328 | tf_op jit(solution)/shard_map/ppermute | solution.py:26
  10.1 9.9 %collective-permute-start.32 = (f32[544]{0:T(1024)S(1)}, f32[544]{0:T(1024)S(1)}, u32[]{:S(2)}, u32[]{:S(2)}) collective-permute-start(f32[544]{0:T(1024)S(1)} %dynamic_slice.150), channel_id=1, source_target_pairs={{0,1},{1,0},{2,3},{3,2},{4,5},{5,4},{6,7},{7,6},{8,9},{9,8},{10,11... | collective-permute-start | bytes 6536 | tf_op jit(solution)/shard_map/ppermute | solution.py:26
  11.0 18.4 %collective-permute-start.5 = (bf16[136,272]{1,0:T(8,128)(2,1)}, bf16[136,272]{1,0:T(8,128)(2,1)}, u32[]{:S(2)}, u32[]{:S(2)}) collective-permute-start(bf16[136,272]{1,0:T(8,128)(2,1)} %copy.72), channel_id=1, source_target_pairs={{0,6},{2,4},{4,2},{6,0},{1,7},{3,5},{5,3},{7,1},{8,14},{10,12},{12... | collective-permute-start | bytes 221960 | tf_op jit(solution)/shard_map/ppermute | solution.py:26
  15.5 24.7 %collective-permute-start.27 = (bf16[136,544]{1,0:T(8,128)(2,1)}, bf16[136,544]{1,0:T(8,128)(2,1)S(1)}, u32[]{:S(2)}, u32[]{:S(2)}) collective-permute-start(bf16[136,544]{1,0:T(8,128)(2,1)} %get-tuple-element.144), channel_id=1, source_target_pairs={{0,6},{2,4},{4,2},{6,0},{1,7},{3,5},{5,3},{7,1},{8,14},{10,12},{12... | collective-permute-start | bytes 443912 | tf_op jit(solution)/shard_map/ppermute | solution.py:26
  20.1 17.6 %collective-permute-start.4 = (bf16[136,272]{1,0:T(8,128)(2,1)}, bf16[136,272]{1,0:T(8,128)(2,1)}, u32[]{:S(2)}, u32[]{:S(2)}) collective-permute-start(bf16[136,272]{1,0:T(8,128)(2,1)} %copy.72), channel_id=1, source_target_pairs={{0,4},{2,6},{4,0},{6,2},{1,5},{3,7},{5,1},{7,3},{8,12},{10,14},{12... | collective-permute-start | bytes 221960 | tf_op jit(solution)/shard_map/ppermute | solution.py:26
  21.2 18.9 %collective-permute-start.3 = (bf16[136,272]{1,0:T(8,128)(2,1)}, bf16[136,272]{1,0:T(8,128)(2,1)}, u32[]{:S(2)}, u32[]{:S(2)}) collective-permute-start(bf16[136,272]{1,0:T(8,128)(2,1)} %copy.72), channel_id=1, source_target_pairs={{0,2},{2,0},{4,6},{6,4},{1,3},{3,1},{5,7},{7,5},{8,10},{10,8},{12,... | collective-permute-start | bytes 221960 | tf_op jit(solution)/shard_map/ppermute | solution.py:26
  26.8 40.3 %collective-permute-start.1 = (bf16[272,512]{1,0:T(8,128)(2,1)S(1)}, bf16[272,512]{1,0:T(8,128)(2,1)S(1)}, u32[]{:S(2)}, u32[]{:S(2)}) collective-permute-start(bf16[272,512]{1,0:T(8,128)(2,1)S(1)} %copy-done.32), channel_id=1, source_target_pairs={{0,4},{2,6},{4,0},{6,2},{1,5},{3,7},{5,1},{7,3},{8,12},{10,14},{12... | collective-permute-start | bytes 835592 | tf_op jit(solution)/shard_map/ppermute | solution.py:26
  29.4 39.6 %collective-permute-start = (bf16[272,512]{1,0:T(8,128)(2,1)S(1)}, bf16[272,512]{1,0:T(8,128)(2,1)S(1)}, u32[]{:S(2)}, u32[]{:S(2)}) collective-permute-start(bf16[272,512]{1,0:T(8,128)(2,1)S(1)} %copy-done.32), channel_id=1, source_target_pairs={{0,2},{2,0},{4,6},{6,4},{1,3},{3,1},{5,7},{7,5},{8,10},{10,8},{12,... | collective-permute-start | bytes 835592 | tf_op jit(solution)/shard_map/ppermute | solution.py:26
  37.7 31.3 %collective-permute-start.2 = (bf16[272,512]{1,0:T(8,128)(2,1)S(1)}, bf16[272,512]{1,0:T(8,128)(2,1)S(1)}, u32[]{:S(2)}, u32[]{:S(2)}) collective-permute-start(bf16[272,512]{1,0:T(8,128)(2,1)S(1)} %copy-done.32), channel_id=1, source_target_pairs={{0,6},{2,4},{4,2},{6,0},{1,7},{3,5},{5,3},{7,1},{8,14},{10,12},{12... | collective-permute-start | bytes 835592 | tf_op jit(solution)/shard_map/ppermute | solution.py:26
  40.1 23.2 %collective-permute-start.26 = (bf16[136,544]{1,0:T(8,128)(2,1)}, bf16[136,544]{1,0:T(8,128)(2,1)}, u32[]{:S(2)}, u32[]{:S(2)}) collective-permute-start(bf16[136,544]{1,0:T(8,128)(2,1)} %get-tuple-element.145), channel_id=1, source_target_pairs={{0,4},{2,6},{4,0},{6,2},{1,5},{3,7},{5,1},{7,3},{8,12},{10,14},{12... | collective-permute-start | bytes 443912 | tf_op jit(solution)/shard_map/ppermute | solution.py:26
  40.2 25.7 %collective-permute-start.25 = (bf16[136,544]{1,0:T(8,128)(2,1)}, bf16[136,544]{1,0:T(8,128)(2,1)}, u32[]{:S(2)}, u32[]{:S(2)}) collective-permute-start(bf16[136,544]{1,0:T(8,128)(2,1)} %get-tuple-element.146), channel_id=1, source_target_pairs={{0,2},{2,0},{4,6},{6,4},{1,3},{3,1},{5,7},{7,5},{8,10},{10,8},{12,... | collective-permute-start | bytes 443912 | tf_op jit(solution)/shard_map/ppermute | solution.py:26
  63.4 35.7 %collective-permute-start.38 = (bf16[272,512]{1,0:T(8,128)(2,1)}, bf16[272,512]{1,0:T(8,128)(2,1)S(1)}, u32[]{:S(2)}, u32[]{:S(2)}) collective-permute-start(bf16[272,512]{1,0:T(8,128)(2,1)} %param.29), channel_id=1, source_target_pairs={{0,6},{2,4},{4,2},{6,0},{1,7},{3,5},{5,3},{7,1},{8,14},{10,12},{12... | collective-permute-start | bytes 835592 | tf_op jit(solution)/shard_map/ppermute | solution.py:26
  65.9 23.4 %collective-permute-start.37 = (bf16[272,512]{1,0:T(8,128)(2,1)}, bf16[272,512]{1,0:T(8,128)(2,1)S(1)}, u32[]{:S(2)}, u32[]{:S(2)}) collective-permute-start(bf16[272,512]{1,0:T(8,128)(2,1)} %param.29), channel_id=1, source_target_pairs={{0,4},{2,6},{4,0},{6,2},{1,5},{3,7},{5,1},{7,3},{8,12},{10,14},{12... | collective-permute-start | bytes 835592 | tf_op jit(solution)/shard_map/ppermute | solution.py:26
  67.1 17.3 %collective-permute-start.36 = (bf16[272,512]{1,0:T(8,128)(2,1)}, bf16[272,512]{1,0:T(8,128)(2,1)S(1)}, u32[]{:S(2)}, u32[]{:S(2)}) collective-permute-start(bf16[272,512]{1,0:T(8,128)(2,1)} %param.29), channel_id=1, source_target_pairs={{0,2},{2,0},{4,6},{6,4},{1,3},{3,1},{5,7},{7,5},{8,10},{10,8},{12,... | collective-permute-start | bytes 835592 | tf_op jit(solution)/shard_map/ppermute | solution.py:26
  69.0 15.8 %collective-permute-start.10 = (bf16[272,544]{1,0:T(8,128)(2,1)}, bf16[272,544]{1,0:T(8,128)(2,1)S(1)}, u32[]{:S(2)}, u32[]{:S(2)}) collective-permute-start(bf16[272,544]{1,0:T(8,128)(2,1)} %constant_dynamic-slice_fusion.15), channel_id=1, source_target_pairs={{0,1},{1,0},{2,3},{3,2},{4,5},{5,4},{6,7},{7,6},{8,9},{9,8},{10,11... | collective-permute-start | bytes 887816 | tf_op jit(solution)/shard_map/ppermute | solution.py:26
  69.0 52.4 %collective-permute-start.8 = (bf16[136,1088]{1,0:T(8,128)(2,1)}, bf16[136,1088]{1,0:T(8,128)(2,1)S(1)}, u32[]{:S(2)}, u32[]{:S(2)}) collective-permute-start(bf16[136,1088]{1,0:T(8,128)(2,1)} %concatenate.133), channel_id=1, source_target_pairs={{0,8},{8,0},{16,24},{24,16},{1,9},{9,1},{17,25},{25,17},{2,10},{10... | collective-permute-start | bytes 887816 | tf_op jit(solution)/shard_map/ppermute | solution.py:26
  90.9 31.0 %collective-permute-start.7 = (bf16[136,1088]{1,0:T(8,128)(2,1)S(1)}, bf16[136,1088]{1,0:T(8,128)(2,1)S(1)}, u32[]{:S(2)}, u32[]{:S(2)}) collective-permute-start(bf16[136,1088]{1,0:T(8,128)(2,1)S(1)} %copy-done.58), channel_id=1, source_target_pairs={{0,16},{8,24},{16,0},{24,8},{1,17},{9,25},{17,1},{25,9},{2,18},{10... | collective-permute-start | bytes 887816 | tf_op jit(solution)/shard_map/ppermute | solution.py:26
  95.9 9.7 %collective-permute-start.16 = (bf16[1088,128]{1,0:T(8,128)(2,1)S(1)}, bf16[1088,128]{1,0:T(8,128)(2,1)S(1)}, u32[]{:S(2)}, u32[]{:S(2)}) collective-permute-start(bf16[1088,128]{1,0:T(8,128)(2,1)S(1)} %pad_maximum_fusion.16), channel_id=1, source_target_pairs={{0,8},{8,0},{16,24},{24,16},{1,9},{9,1},{17,25},{25,17},{2,10},{10... | collective-permute-start | bytes 835592 | tf_op jit(solution)/shard_map/ppermute | solution.py:26
  97.5 20.3 %collective-permute-start.15 = (bf16[1088,128]{1,0:T(8,128)(2,1)S(1)}, bf16[1088,128]{1,0:T(8,128)(2,1)S(1)}, u32[]{:S(2)}, u32[]{:S(2)}) collective-permute-start(bf16[1088,128]{1,0:T(8,128)(2,1)S(1)} %pad_maximum_fusion.16), channel_id=1, source_target_pairs={{0,16},{8,24},{16,0},{24,8},{1,17},{9,25},{17,1},{25,9},{2,18},{10... | collective-permute-start | bytes 835592 | tf_op jit(solution)/shard_map/ppermute | solution.py:26
  99.0 20.3 %collective-permute-start.14 = (bf16[1088,128]{1,0:T(8,128)(2,1)S(1)}, bf16[1088,128]{1,0:T(8,128)(2,1)S(1)}, u32[]{:S(2)}, u32[]{:S(2)}) collective-permute-start(bf16[1088,128]{1,0:T(8,128)(2,1)S(1)} %pad_maximum_fusion.16), channel_id=1, source_target_pairs={{0,24},{8,16},{16,8},{24,0},{1,25},{9,17},{17,9},{25,1},{2,26},{10... | collective-permute-start | bytes 835592 | tf_op jit(solution)/shard_map/ppermute | solution.py:26
  105.6 16.3 %collective-permute-start.6 = (bf16[136,1088]{1,0:T(8,128)(2,1)S(1)}, bf16[136,1088]{1,0:T(8,128)(2,1)S(1)}, u32[]{:S(2)}, u32[]{:S(2)}) collective-permute-start(bf16[136,1088]{1,0:T(8,128)(2,1)S(1)} %copy-done.58), channel_id=1, source_target_pairs={{0,24},{8,16},{16,8},{24,0},{1,25},{9,17},{17,9},{25,1},{2,26},{10... | collective-permute-start | bytes 887816 | tf_op jit(solution)/shard_map/ppermute | solution.py:26
  117.8 18.5 %collective-permute-start.30 = (bf16[4,136,544]{2,1,0:T(8,128)(2,1)S(1)}, bf16[4,136,544]{2,1,0:T(8,128)(2,1)S(1)}, u32[]{:S(2)}, u32[]{:S(2)}) collective-permute-start(bf16[4,136,544]{2,1,0:T(8,128)(2,1)S(1)} %pad_maximum_fusion.15), channel_id=1, source_target_pairs={{0,8},{8,0},{16,24},{24,16},{1,9},{9,1},{17,25},{25,17},{2,10},{10... | collective-permute-start | bytes 1775624 | tf_op jit(solution)/shard_map/ppermute | solution.py:26
  119.3 29.1 %collective-permute-start.29 = (bf16[4,136,544]{2,1,0:T(8,128)(2,1)S(1)}, bf16[4,136,544]{2,1,0:T(8,128)(2,1)S(1)}, u32[]{:S(2)}, u32[]{:S(2)}) collective-permute-start(bf16[4,136,544]{2,1,0:T(8,128)(2,1)S(1)} %pad_maximum_fusion.15), channel_id=1, source_target_pairs={{0,16},{8,24},{16,0},{24,8},{1,17},{9,25},{17,1},{25,9},{2,18},{10... | collective-permute-start | bytes 1775624 | tf_op jit(solution)/shard_map/ppermute | solution.py:26
  121.4 28.6 %collective-permute-start.28 = (bf16[4,136,544]{2,1,0:T(8,128)(2,1)S(1)}, bf16[4,136,544]{2,1,0:T(8,128)(2,1)S(1)}, u32[]{:S(2)}, u32[]{:S(2)}) collective-permute-start(bf16[4,136,544]{2,1,0:T(8,128)(2,1)S(1)} %pad_maximum_fusion.15), channel_id=1, source_target_pairs={{0,24},{8,16},{16,8},{24,0},{1,25},{9,17},{17,9},{25,1},{2,26},{10... | collective-permute-start | bytes 1775624 | tf_op jit(solution)/shard_map/ppermute | solution.py:26
  121.9 31.0 %collective-permute-start.17 = (bf16[1088,512]{1,0:T(8,128)(2,1)S(1)}, bf16[1088,512]{1,0:T(8,128)(2,1)S(1)}, u32[]{:S(2)}, u32[]{:S(2)}) collective-permute-start(bf16[1088,512]{1,0:T(8,128)(2,1)S(1)} %pad_maximum_fusion.13), channel_id=1, source_target_pairs={{0,1},{1,0},{2,3},{3,2},{4,5},{5,4},{6,7},{7,6},{8,9},{9,8},{10,11... | collective-permute-start | bytes 3342344 | tf_op jit(solution)/shard_map/ppermute | solution.py:26
  123.4 77.6 %collective-permute-start.9 = (bf16[544,1088]{1,0:T(8,128)(2,1)}, bf16[544,1088]{1,0:T(8,128)(2,1)}, u32[]{:S(2)}, u32[]{:S(2)}) collective-permute-start(bf16[544,1088]{1,0:T(8,128)(2,1)} %pad_maximum_fusion.11), channel_id=1, source_target_pairs={{0,1},{1,0},{2,3},{3,2},{4,5},{5,4},{6,7},{7,6},{8,9},{9,8},{10,11... | collective-permute-start | bytes 3551240 | tf_op jit(solution)/shard_map/ppermute | solution.py:26
  164.1 12.6 %collective-permute-start.21 = (bf16[640,512]{1,0:T(8,128)(2,1)S(1)}, bf16[640,512]{1,0:T(8,128)(2,1)}, u32[]{:S(2)}, u32[]{:S(2)}) collective-permute-start(bf16[640,512]{1,0:T(8,128)(2,1)S(1)} %slice.458), channel_id=1, source_target_pairs={{0,1},{1,0},{2,3},{3,2},{4,5},{5,4},{6,7},{7,6},{8,9},{9,8},{10,11... | collective-permute-start | bytes 1966088 | tf_op jit(solution)/shard_map/ppermute | solution.py:26
  174.1 61.5 %collective-permute-start.31 = (bf16[2,1088,544]{1,2,0:T(8,128)(2,1)}, bf16[2,1088,544]{1,2,0:T(8,128)(2,1)}, u32[]{:S(2)}, u32[]{:S(2)}) collective-permute-start(bf16[2,1088,544]{1,2,0:T(8,128)(2,1)} %copy.60), channel_id=1, source_target_pairs={{0,1},{1,0},{2,3},{3,2},{4,5},{5,4},{6,7},{7,6},{8,9},{9,8},{10,11... | collective-permute-start | bytes 7102472 | tf_op jit(solution)/shard_map/ppermute | solution.py:26
  196.5 13.8 %collective-permute-start.24 = (bf16[272,512]{1,0:T(8,128)(2,1)S(1)}, bf16[272,512]{1,0:T(8,128)(2,1)S(1)}, u32[]{:S(2)}, u32[]{:S(2)}) collective-permute-start(bf16[272,512]{1,0:T(8,128)(2,1)S(1)} %pad_maximum_fusion.17), channel_id=1, source_target_pairs={{0,2},{2,0},{4,6},{6,4},{1,3},{3,1},{5,7},{7,5},{8,10},{10,8},{12,... | collective-permute-start | bytes 835592 | tf_op jit(solution)/shard_map/ppermute | solution.py:26
  197.5 22.4 %collective-permute-start.23 = (bf16[272,512]{1,0:T(8,128)(2,1)S(1)}, bf16[272,512]{1,0:T(8,128)(2,1)S(1)}, u32[]{:S(2)}, u32[]{:S(2)}) collective-permute-start(bf16[272,512]{1,0:T(8,128)(2,1)S(1)} %pad_maximum_fusion.17), channel_id=1, source_target_pairs={{0,4},{2,6},{4,0},{6,2},{1,5},{3,7},{5,1},{7,3},{8,12},{10,14},{12... | collective-permute-start | bytes 835592 | tf_op jit(solution)/shard_map/ppermute | solution.py:26
  199.1 20.8 %collective-permute-start.22 = (bf16[272,512]{1,0:T(8,128)(2,1)S(1)}, bf16[272,512]{1,0:T(8,128)(2,1)S(1)}, u32[]{:S(2)}, u32[]{:S(2)}) collective-permute-start(bf16[272,512]{1,0:T(8,128)(2,1)S(1)} %pad_maximum_fusion.17), channel_id=1, source_target_pairs={{0,6},{2,4},{4,2},{6,0},{1,7},{3,5},{5,3},{7,1},{8,14},{10,12},{12... | collective-permute-start | bytes 835592 | tf_op jit(solution)/shard_map/ppermute | solution.py:26
  267.5 58.6 %collective-permute-start.35 = (bf16[272,512]{1,0:T(8,128)(2,1)}, bf16[272,512]{1,0:T(8,128)(2,1)}, u32[]{:S(2)}, u32[]{:S(2)}) collective-permute-start(bf16[272,512]{1,0:T(8,128)(2,1)} %get-tuple-element.126), channel_id=1, source_target_pairs={{0,6},{2,4},{4,2},{6,0},{1,7},{3,5},{5,3},{7,1},{8,14},{10,12},{12... | collective-permute-start | bytes 835592 | tf_op jit(solution)/shard_map/ppermute | solution.py:26
  270.0 14.4 %collective-permute-start.39 = (bf16[1088,128]{1,0:T(8,128)(2,1)}, bf16[1088,128]{1,0:T(8,128)(2,1)}, u32[]{:S(2)}, u32[]{:S(2)}) collective-permute-start(bf16[1088,128]{1,0:T(8,128)(2,1)} %get-tuple-element.122), channel_id=1, source_target_pairs={{0,2},{2,0},{4,6},{6,4},{1,3},{3,1},{5,7},{7,5},{8,10},{10,8},{12,... | collective-permute-start | bytes 835592 | tf_op jit(solution)/shard_map/ppermute | solution.py:26
  275.3 16.4 %collective-permute-start.41 = (bf16[1088,128]{1,0:T(8,128)(2,1)S(1)}, bf16[1088,128]{1,0:T(8,128)(2,1)}, u32[]{:S(2)}, u32[]{:S(2)}) collective-permute-start(bf16[1088,128]{1,0:T(8,128)(2,1)S(1)} %get-tuple-element.123), channel_id=1, source_target_pairs={{0,6},{2,4},{4,2},{6,0},{1,7},{3,5},{5,3},{7,1},{8,14},{10,12},{12... | collective-permute-start | bytes 835592 | tf_op jit(solution)/shard_map/ppermute | solution.py:26
  281.6 42.5 %collective-permute-start.33 = (bf16[272,512]{1,0:T(8,128)(2,1)}, bf16[272,512]{1,0:T(8,128)(2,1)S(1)}, u32[]{:S(2)}, u32[]{:S(2)}) collective-permute-start(bf16[272,512]{1,0:T(8,128)(2,1)} %get-tuple-element.125), channel_id=1, source_target_pairs={{0,2},{2,0},{4,6},{6,4},{1,3},{3,1},{5,7},{7,5},{8,10},{10,8},{12,... | collective-permute-start | bytes 835592 | tf_op jit(solution)/shard_map/ppermute | solution.py:26
  281.6 46.9 %collective-permute-start.34 = (bf16[272,512]{1,0:T(8,128)(2,1)}, bf16[272,512]{1,0:T(8,128)(2,1)S(1)}, u32[]{:S(2)}, u32[]{:S(2)}) collective-permute-start(bf16[272,512]{1,0:T(8,128)(2,1)} %get-tuple-element.127), channel_id=1, source_target_pairs={{0,4},{2,6},{4,0},{6,2},{1,5},{3,7},{5,1},{7,3},{8,12},{10,14},{12... | collective-permute-start | bytes 835592 | tf_op jit(solution)/shard_map/ppermute | solution.py:26
  284.4 34.1 %collective-permute-start.40 = (bf16[1088,128]{1,0:T(8,128)(2,1)S(1)}, bf16[1088,128]{1,0:T(8,128)(2,1)S(1)}, u32[]{:S(2)}, u32[]{:S(2)}) collective-permute-start(bf16[1088,128]{1,0:T(8,128)(2,1)S(1)} %get-tuple-element.124), channel_id=1, source_target_pairs={{0,4},{2,6},{4,0},{6,2},{1,5},{3,7},{5,1},{7,3},{8,12},{10,14},{12... | collective-permute-start | bytes 835592 | tf_op jit(solution)/shard_map/ppermute | solution.py:26
  291.6 148.5 %collective-permute-start.75 = (bf16[2,1088,544]{1,2,0:T(8,128)(2,1)}, bf16[2,1088,544]{1,2,0:T(8,128)(2,1)}, u32[]{:S(2)}, u32[]{:S(2)}) collective-permute-start(bf16[2,1088,544]{1,2,0:T(8,128)(2,1)} %pad_maximum_fusion.6), channel_id=1, source_target_pairs={{0,1},{1,0},{2,3},{3,2},{4,5},{5,4},{6,7},{7,6},{8,9},{9,8},{10,11... | collective-permute-start | bytes 7102472 | tf_op jit(solution)/shard_map/ppermute | solution.py:26
  331.3 10.9 %collective-permute-start.44 = (bf16[272,128]{1,0:T(8,128)(2,1)S(1)}, bf16[272,128]{1,0:T(8,128)(2,1)S(1)}, u32[]{:S(2)}, u32[]{:S(2)}) collective-permute-start(bf16[272,128]{1,0:T(8,128)(2,1)S(1)} %get-tuple-element.187), channel_id=1, source_target_pairs={{0,2},{2,0},{4,6},{6,4},{1,3},{3,1},{5,7},{7,5},{8,10},{10,8},{12,... | collective-permute-start | bytes 208904 | tf_op jit(solution)/shard_map/ppermute | solution.py:26
  331.3 10.9 %collective-permute-start.43 = (bf16[272,128]{1,0:T(8,128)(2,1)S(1)}, bf16[272,128]{1,0:T(8,128)(2,1)S(1)}, u32[]{:S(2)}, u32[]{:S(2)}) collective-permute-start(bf16[272,128]{1,0:T(8,128)(2,1)S(1)} %get-tuple-element.188), channel_id=1, source_target_pairs={{0,4},{2,6},{4,0},{6,2},{1,5},{3,7},{5,1},{7,3},{8,12},{10,14},{12... | collective-permute-start | bytes 208904 | tf_op jit(solution)/shard_map/ppermute | solution.py:26
  352.5 12.6 %collective-permute-start.48 = (bf16[640,512]{1,0:T(8,128)(2,1)}, bf16[640,512]{1,0:T(8,128)(2,1)}, u32[]{:S(2)}, u32[]{:S(2)}) collective-permute-start(bf16[640,512]{1,0:T(8,128)(2,1)} %slice.689), channel_id=1, source_target_pairs={{0,1},{1,0},{2,3},{3,2},{4,5},{5,4},{6,7},{7,6},{8,9},{9,8},{10,11... | collective-permute-start | bytes 1966088 | tf_op jit(solution)/shard_map/ppermute | solution.py:26
  380.8 17.2 %collective-permute-start.57 = (bf16[1088,512]{1,0:T(8,128)(2,1)S(1)}, bf16[1088,512]{1,0:T(8,128)(2,1)S(1)}, u32[]{:S(2)}, u32[]{:S(2)}) collective-permute-start(bf16[1088,512]{1,0:T(8,128)(2,1)S(1)} %select_convert_fusion), channel_id=1, source_target_pairs={{0,1},{1,0},{2,3},{3,2},{4,5},{5,4},{6,7},{7,6},{8,9},{9,8},{10,11... | collective-permute-start | bytes 3342344 | tf_op jit(solution)/shard_map/ppermute | solution.py:26
  400.7 10.9 %collective-permute-start.60 = (bf16[1088,128]{1,0:T(8,128)(2,1)S(1)}, bf16[1088,128]{1,0:T(8,128)(2,1)S(1)}, u32[]{:S(2)}, u32[]{:S(2)}) collective-permute-start(bf16[1088,128]{1,0:T(8,128)(2,1)S(1)} %get-tuple-element.117), channel_id=1, source_target_pairs={{0,24},{8,16},{16,8},{24,0},{1,25},{9,17},{17,9},{25,1},{2,26},{10... | collective-permute-start | bytes 835592 | tf_op jit(solution)/shard_map/ppermute | solution.py:26
  402.2 11.0 %collective-permute-start.59 = (bf16[1088,128]{1,0:T(8,128)(2,1)S(1)}, bf16[1088,128]{1,0:T(8,128)(2,1)S(1)}, u32[]{:S(2)}, u32[]{:S(2)}) collective-permute-start(bf16[1088,128]{1,0:T(8,128)(2,1)S(1)} %get-tuple-element.118), channel_id=1, source_target_pairs={{0,16},{8,24},{16,0},{24,8},{1,17},{9,25},{17,1},{25,9},{2,18},{10... | collective-permute-start | bytes 835592 | tf_op jit(solution)/shard_map/ppermute | solution.py:26
  403.4 11.7 %collective-permute-start.49 = (bf16[272,512]{1,0:T(8,128)(2,1)S(1)}, bf16[272,512]{1,0:T(8,128)(2,1)S(1)}, u32[]{:S(2)}, u32[]{:S(2)}) collective-permute-start(bf16[272,512]{1,0:T(8,128)(2,1)S(1)} %get-tuple-element.119), channel_id=1, source_target_pairs={{0,2},{2,0},{4,6},{6,4},{1,3},{3,1},{5,7},{7,5},{8,10},{10,8},{12,... | collective-permute-start | bytes 835592 | tf_op jit(solution)/shard_map/ppermute | solution.py:26
  408.1 11.4 %collective-permute-start.51 = (bf16[272,512]{1,0:T(8,128)(2,1)S(1)}, bf16[272,512]{1,0:T(8,128)(2,1)S(1)}, u32[]{:S(2)}, u32[]{:S(2)}) collective-permute-start(bf16[272,512]{1,0:T(8,128)(2,1)S(1)} %get-tuple-element.120), channel_id=1, source_target_pairs={{0,6},{2,4},{4,2},{6,0},{1,7},{3,5},{5,3},{7,1},{8,14},{10,12},{12... | collective-permute-start | bytes 835592 | tf_op jit(solution)/shard_map/ppermute | solution.py:26
  411.6 22.1 %collective-permute-start.50 = (bf16[272,512]{1,0:T(8,128)(2,1)S(1)}, bf16[272,512]{1,0:T(8,128)(2,1)S(1)}, u32[]{:S(2)}, u32[]{:S(2)}) collective-permute-start(bf16[272,512]{1,0:T(8,128)(2,1)S(1)} %get-tuple-element.121), channel_id=1, source_target_pairs={{0,4},{2,6},{4,0},{6,2},{1,5},{3,7},{5,1},{7,3},{8,12},{10,14},{12... | collective-permute-start | bytes 835592 | tf_op jit(solution)/shard_map/ppermute | solution.py:26
  414.5 21.3 %collective-permute-start.63 = (bf16[272,128]{1,0:T(8,128)(2,1)S(1)}, bf16[272,128]{1,0:T(8,128)(2,1)S(1)}, u32[]{:S(2)}, u32[]{:S(2)}) collective-permute-start(bf16[272,128]{1,0:T(8,128)(2,1)S(1)} %get-tuple-element.184), channel_id=1, source_target_pairs={{0,2},{2,0},{4,6},{6,4},{1,3},{3,1},{5,7},{7,5},{8,10},{10,8},{12,... | collective-permute-start | bytes 208904 | tf_op jit(solution)/shard_map/ppermute | solution.py:26
  415.0 20.8 %collective-permute-start.62 = (bf16[272,128]{1,0:T(8,128)(2,1)S(1)}, bf16[272,128]{1,0:T(8,128)(2,1)S(1)}, u32[]{:S(2)}, u32[]{:S(2)}) collective-permute-start(bf16[272,128]{1,0:T(8,128)(2,1)S(1)} %get-tuple-element.185), channel_id=1, source_target_pairs={{0,4},{2,6},{4,0},{6,2},{1,5},{3,7},{5,1},{7,3},{8,12},{10,14},{12... | collective-permute-start | bytes 208904 | tf_op jit(solution)/shard_map/ppermute | solution.py:26
  419.5 16.3 %collective-permute-start.61 = (bf16[272,128]{1,0:T(8,128)(2,1)S(1)}, bf16[272,128]{1,0:T(8,128)(2,1)S(1)}, u32[]{:S(2)}, u32[]{:S(2)}) collective-permute-start(bf16[272,128]{1,0:T(8,128)(2,1)S(1)} %get-tuple-element.186), channel_id=1, source_target_pairs={{0,6},{2,4},{4,2},{6,0},{1,7},{3,5},{5,3},{7,1},{8,14},{10,12},{12... | collective-permute-start | bytes 208904 | tf_op jit(solution)/shard_map/ppermute | solution.py:26
  436.6 14.6 %collective-permute-start.66 = (bf16[4,272,128]{2,1,0:T(8,128)(2,1)}, bf16[4,272,128]{2,1,0:T(8,128)(2,1)S(1)}, u32[]{:S(2)}, u32[]{:S(2)}) collective-permute-start(bf16[4,272,128]{2,1,0:T(8,128)(2,1)} %pad_maximum_fusion.19), channel_id=1, source_target_pairs={{0,8},{8,0},{16,24},{24,16},{1,9},{9,1},{17,25},{25,17},{2,10},{10... | collective-permute-start | bytes 835592 | tf_op jit(solution)/shard_map/ppermute | solution.py:26
  437.5 14.7 %collective-permute-start.65 = (bf16[4,272,128]{2,1,0:T(8,128)(2,1)}, bf16[4,272,128]{2,1,0:T(8,128)(2,1)}, u32[]{:S(2)}, u32[]{:S(2)}) collective-permute-start(bf16[4,272,128]{2,1,0:T(8,128)(2,1)} %pad_maximum_fusion.19), channel_id=1, source_target_pairs={{0,16},{8,24},{16,0},{24,8},{1,17},{9,25},{17,1},{25,9},{2,18},{10... | collective-permute-start | bytes 835592 | tf_op jit(solution)/shard_map/ppermute | solution.py:26
  438.5 13.7 %collective-permute-start.64 = (bf16[4,272,128]{2,1,0:T(8,128)(2,1)}, bf16[4,272,128]{2,1,0:T(8,128)(2,1)}, u32[]{:S(2)}, u32[]{:S(2)}) collective-permute-start(bf16[4,272,128]{2,1,0:T(8,128)(2,1)} %pad_maximum_fusion.19), channel_id=1, source_target_pairs={{0,24},{8,16},{16,8},{24,0},{1,25},{9,17},{17,9},{25,1},{2,26},{10... | collective-permute-start | bytes 835592 | tf_op jit(solution)/shard_map/ppermute | solution.py:26
  448.7 18.6 %collective-permute-start.76 = (bf16[4,136,544]{2,1,0:T(8,128)(2,1)S(1)}, bf16[4,136,544]{2,1,0:T(8,128)(2,1)S(1)}, u32[]{:S(2)}, u32[]{:S(2)}) collective-permute-start(bf16[4,136,544]{2,1,0:T(8,128)(2,1)S(1)} %get-tuple-element.89), channel_id=1, source_target_pairs={{0,8},{8,0},{16,24},{24,16},{1,9},{9,1},{17,25},{25,17},{2,10},{10... | collective-permute-start | bytes 1775624 | tf_op jit(solution)/shard_map/ppermute | solution.py:26
  449.7 27.2 %collective-permute-start.78 = (bf16[4,136,544]{2,1,0:T(8,128)(2,1)S(1)}, bf16[4,136,544]{2,1,0:T(8,128)(2,1)S(1)}, u32[]{:S(2)}, u32[]{:S(2)}) collective-permute-start(bf16[4,136,544]{2,1,0:T(8,128)(2,1)S(1)} %get-tuple-element.90), channel_id=1, source_target_pairs={{0,24},{8,16},{16,8},{24,0},{1,25},{9,17},{17,9},{25,1},{2,26},{10... | collective-permute-start | bytes 1775624 | tf_op jit(solution)/shard_map/ppermute | solution.py:26
  451.2 26.3 %collective-permute-start.77 = (bf16[4,136,544]{2,1,0:T(8,128)(2,1)S(1)}, bf16[4,136,544]{2,1,0:T(8,128)(2,1)S(1)}, u32[]{:S(2)}, u32[]{:S(2)}) collective-permute-start(bf16[4,136,544]{2,1,0:T(8,128)(2,1)S(1)} %get-tuple-element.91), channel_id=1, source_target_pairs={{0,16},{8,24},{16,0},{24,8},{1,17},{9,25},{17,1},{25,9},{2,18},{10... | collective-permute-start | bytes 1775624 | tf_op jit(solution)/shard_map/ppermute | solution.py:26
  454.2 28.9 %collective-permute-start.67 = (bf16[4,272,128]{2,1,0:T(8,128)(2,1)S(1)}, bf16[4,272,128]{2,1,0:T(8,128)(2,1)S(1)}, u32[]{:S(2)}, u32[]{:S(2)}) collective-permute-start(bf16[4,272,128]{2,1,0:T(8,128)(2,1)S(1)} %get-tuple-element.113), channel_id=1, source_target_pairs={{0,1},{1,0},{2,3},{3,2},{4,5},{5,4},{6,7},{7,6},{8,9},{9,8},{10,11... | collective-permute-start | bytes 835592 | tf_op jit(solution)/shard_map/ppermute | solution.py:26
  478.7 10.7 %collective-permute-start.81 = (bf16[136,544]{1,0:T(8,128)(2,1)}, bf16[136,544]{1,0:T(8,128)(2,1)}, u32[]{:S(2)}, u32[]{:S(2)}) collective-permute-start(bf16[136,544]{1,0:T(8,128)(2,1)} %get-tuple-element.135), channel_id=1, source_target_pairs={{0,2},{2,0},{4,6},{6,4},{1,3},{3,1},{5,7},{7,5},{8,10},{10,8},{12,... | collective-permute-start | bytes 443912 | tf_op jit(solution)/shard_map/ppermute | solution.py:26
  480.1 11.7 %collective-permute-start.80 = (bf16[136,544]{1,0:T(8,128)(2,1)}, bf16[136,544]{1,0:T(8,128)(2,1)}, u32[]{:S(2)}, u32[]{:S(2)}) collective-permute-start(bf16[136,544]{1,0:T(8,128)(2,1)} %get-tuple-element.136), channel_id=1, source_target_pairs={{0,4},{2,6},{4,0},{6,2},{1,5},{3,7},{5,1},{7,3},{8,12},{10,14},{12... | collective-permute-start | bytes 443912 | tf_op jit(solution)/shard_map/ppermute | solution.py:26
  480.3 11.5 %collective-permute-start.79 = (bf16[136,544]{1,0:T(8,128)(2,1)}, bf16[136,544]{1,0:T(8,128)(2,1)}, u32[]{:S(2)}, u32[]{:S(2)}) collective-permute-start(bf16[136,544]{1,0:T(8,128)(2,1)} %get-tuple-element.137), channel_id=1, source_target_pairs={{0,6},{2,4},{4,2},{6,0},{1,7},{3,5},{5,3},{7,1},{8,14},{10,12},{12... | collective-permute-start | bytes 443912 | tf_op jit(solution)/shard_map/ppermute | solution.py:26
  495.2 14.2 %collective-permute-start.84 = (bf16[136,2176]{1,0:T(8,128)(2,1)S(1)}, bf16[136,2176]{1,0:T(8,128)(2,1)S(1)}, u32[]{:S(2)}, u32[]{:S(2)}) collective-permute-start(bf16[136,2176]{1,0:T(8,128)(2,1)S(1)} %concatenate.169), channel_id=1, source_target_pairs={{0,8},{8,0},{16,24},{24,16},{1,9},{9,1},{17,25},{25,17},{2,10},{10... | collective-permute-start | bytes 1775624 | tf_op jit(solution)/shard_map/ppermute | solution.py:26
  496.1 20.2 %collective-permute-start.83 = (bf16[136,2176]{1,0:T(8,128)(2,1)S(1)}, bf16[136,2176]{1,0:T(8,128)(2,1)S(1)}, u32[]{:S(2)}, u32[]{:S(2)}) collective-permute-start(bf16[136,2176]{1,0:T(8,128)(2,1)S(1)} %concatenate.169), channel_id=1, source_target_pairs={{0,16},{8,24},{16,0},{24,8},{1,17},{9,25},{17,1},{25,9},{2,18},{10... | collective-permute-start | bytes 1775624 | tf_op jit(solution)/shard_map/ppermute | solution.py:26
  497.1 19.1 %collective-permute-start.82 = (bf16[136,2176]{1,0:T(8,128)(2,1)S(1)}, bf16[136,2176]{1,0:T(8,128)(2,1)S(1)}, u32[]{:S(2)}, u32[]{:S(2)}) collective-permute-start(bf16[136,2176]{1,0:T(8,128)(2,1)S(1)} %concatenate.169), channel_id=1, source_target_pairs={{0,24},{8,16},{16,8},{24,0},{1,25},{9,17},{17,9},{25,1},{2,26},{10... | collective-permute-start | bytes 1775624 | tf_op jit(solution)/shard_map/ppermute | solution.py:26
  (140 other events, 1379.5 us)
